TPU v7x, 128 devices: a whole 4x4x4 slice. The times are simulated.
128 devices in a mesh: lat: 8 (over z_hi, y), lon: 16 (over x, z_lo, core).
Axes of the slice: x: 4, y: 4, z: 4 (z_hi: 2, z_lo: 2; z = z_hi * 2 + z_lo), core: 2. Of those that a mesh axis runs over, the one named last changes fastest.
Arguments:
- queries: bfloat16 [128, 256, 1024], P(('lat', 'lon')), may hold values from -32 to 32
- keys: bfloat16 [128, 256, 1024], P(('lat', 'lon')), may hold values from -32 to 32
- values: bfloat16 [128, 256, 1024], P(('lat', 'lon')), may hold values from -6 to 6
- grads_out: bfloat16 [128, 256, 1024], P(('lat', 'lon')), may hold values from -6 to 6
Outputs:
- grad_queries: bfloat16 [128, 256, 1024], P('lat', 'lon')
- grad_keys: bfloat16 [128, 256, 1024], P('lat', 'lon')
- grad_values: bfloat16 [128, 256, 1024], P('lat', 'lon')
All inputs are finite; a program needn't handle non-finite values.
Results may differ from a plain program's by a relative error of at most 0.02.
Values may be sent and summed in bfloat16 or wider, within the bound.
A program may use at most 448 MiB of HBM per device.

v0:
```python
import jax
import jax.numpy as jnp
from jax import lax
from jax.sharding import PartitionSpec as P

HEADS = 16
RADIUS = 6
TILE = 8


masked_score = -1e30


def with_halo(block, sides, width, periodic):
    for axis, dim in sides:
        count = lax.axis_size(axis)
        forward = [(i, i + 1) for i in range(count - 1)]
        if periodic:
            forward.append((count - 1, 0))
        backward = [(target, source) for source, target in forward]
        low = lax.ppermute(
            lax.slice_in_dim(block, block.shape[dim] - width, None, axis=dim), axis, forward
        )
        high = lax.ppermute(lax.slice_in_dim(block, 0, width, axis=dim), axis, backward)
        block = jnp.concatenate([low, block, high], axis=dim)
    return block


def window_grads(queries, grads_out, keys, values, key_first, total_rows):
    query_rows, query_cols, features = queries.shape
    tile_cols = query_cols // TILE
    tile_rows = query_rows // TILE
    head_size = features // HEADS
    score_scale = head_size ** (-0.5)
    offsets = jnp.arange(3 * TILE)[None, :] - jnp.arange(TILE)[:, None]
    inside = (offsets >= 0) & (offsets <= 2 * RADIUS)
    allowed = inside[:, None, :, None] & inside[None, :, None, :]

    def one_row(index, carry):
        grad_q, grad_kv = carry
        first_row = (index * TILE).astype(jnp.int32)
        q_tile = lax.dynamic_slice_in_dim(queries, first_row, TILE, 0).reshape(
            TILE, tile_cols, TILE, HEADS, head_size
        )
        d_tile = lax.dynamic_slice_in_dim(grads_out, first_row, TILE, 0).reshape(
            TILE, tile_cols, TILE, HEADS, head_size
        )
        k_rows = lax.dynamic_slice_in_dim(keys, first_row, 3 * TILE, 0).reshape(
            3 * TILE, tile_cols + 2, TILE, HEADS, head_size
        )
        v_rows = lax.dynamic_slice_in_dim(values, first_row, 3 * TILE, 0).reshape(
            3 * TILE, tile_cols + 2, TILE, HEADS, head_size
        )
        k_win = jnp.concatenate(
            [k_rows[:, 0:tile_cols], k_rows[:, 1 : tile_cols + 1], k_rows[:, 2 : tile_cols + 2]],
            axis=2,
        )
        v_win = jnp.concatenate(
            [v_rows[:, 0:tile_cols], v_rows[:, 1 : tile_cols + 1], v_rows[:, 2 : tile_cols + 2]],
            axis=2,
        )
        global_rows = key_first + first_row + jnp.arange(3 * TILE)
        row_ok = (global_rows >= 0) & (global_rows < total_rows)
        valid = allowed & row_ok[None, None, :, None]
        scores = (
            jnp.einsum("acbhe,icjhe->chabij", q_tile, k_win, preferred_element_type=jnp.float32)
            * score_scale
        )
        scores = jnp.where(valid, scores, masked_score)
        top_score = jnp.max(scores, axis=(4, 5), keepdims=True)
        weights = jnp.exp(scores - top_score)
        probs = weights / jnp.sum(weights, axis=(4, 5), keepdims=True)
        probs_low = probs.astype(jnp.bfloat16)
        d_probs = jnp.einsum(
            "acbhe,icjhe->chabij", d_tile, v_win, preferred_element_type=jnp.float32
        )
        centre = jnp.sum(probs * d_probs, axis=(4, 5), keepdims=True)
        d_scores = (probs * (d_probs - centre) * score_scale).astype(jnp.bfloat16)
        dq_tile = jnp.einsum(
            "chabij,icjhe->acbhe", d_scores, k_win, preferred_element_type=jnp.float32
        )
        grad_q = lax.dynamic_update_slice_in_dim(
            grad_q, dq_tile.reshape(TILE, query_cols, features).astype(jnp.bfloat16), first_row, 0
        )
        dk_win = jnp.einsum(
            "chabij,acbhe->icjhe", d_scores, q_tile, preferred_element_type=jnp.float32
        )
        dv_win = jnp.einsum(
            "chabij,acbhe->icjhe", probs_low, d_tile, preferred_element_type=jnp.float32
        )
        both = jnp.stack([dk_win, dv_win]).reshape(
            2, 3 * TILE, tile_cols, 3, TILE, HEADS, head_size
        )
        plain = ((0, 0), (0, 0))
        rest = ((0, 0), (0, 0), (0, 0))
        folded = jnp.pad(both[:, :, :, 0], plain + ((0, 2),) + rest)
        folded = folded + jnp.pad(both[:, :, :, 1], plain + ((1, 1),) + rest)
        folded = folded + jnp.pad(both[:, :, :, 2], plain + ((2, 0),) + rest)
        folded = folded.reshape(2, 3 * TILE, query_cols + 2 * TILE, features)
        current = lax.dynamic_slice_in_dim(grad_kv, first_row, 3 * TILE, 1)
        grad_kv = lax.dynamic_update_slice_in_dim(grad_kv, current + folded, first_row, 1)
        return (grad_q, grad_kv)

    begin = (
        jnp.zeros((query_rows, query_cols, features), jnp.bfloat16),
        jnp.zeros((2, query_rows + 2 * TILE, query_cols + 2 * TILE, features), jnp.float32),
    )
    return lax.fori_loop(0, tile_rows, one_row, begin)


def on_device(queries, keys, values, grads_out):
    queries, keys, values, grads_out = (
        lax.all_to_all(queries, "lon", split_axis=1, concat_axis=0, tiled=True),
        lax.all_to_all(keys, "lon", split_axis=1, concat_axis=0, tiled=True),
        lax.all_to_all(values, "lon", split_axis=1, concat_axis=0, tiled=True),
        lax.all_to_all(grads_out, "lon", split_axis=1, concat_axis=0, tiled=True),
    )
    tile_height, tile_width, features = queries.shape
    total_rows = tile_height * lax.axis_size("lat")
    first_global = lax.axis_index("lat") * tile_height
    spare_cells = 2 * TILE - 2 * RADIUS
    padding = ((0, 0), (0, spare_cells), (0, spare_cells), (0, 0))
    kv_pair = jnp.stack([keys, values])
    nearby = with_halo(kv_pair, (("lat", 1), ("lon", 2)), RADIUS, True)
    nearby = jnp.pad(nearby, padding)
    grad_q, grad_kv = window_grads(
        queries, grads_out, nearby[0], nearby[1], first_global - RADIUS, total_rows
    )
    banded = grad_kv[:, : tile_height + 2 * RADIUS, : tile_width + 2 * RADIUS]
    sides = jnp.concatenate([banded[:, :, :RADIUS], banded[:, :, tile_width + RADIUS :]], axis=2)
    sides = with_halo(sides.astype(jnp.bfloat16), (("lon", 2),), RADIUS, True).astype(sides.dtype)
    middle = banded[:, :, RADIUS : tile_width + RADIUS]
    middle = middle.at[:, :, :RADIUS].add(sides[:, :, :RADIUS])
    middle = middle.at[:, :, tile_width - RADIUS :].add(sides[:, :, 3 * RADIUS :])
    edges = jnp.concatenate([middle[:, :RADIUS], middle[:, tile_height + RADIUS :]], axis=1)
    edges = with_halo(edges.astype(jnp.bfloat16), (("lat", 1),), RADIUS, False).astype(edges.dtype)
    core = middle[:, RADIUS : tile_height + RADIUS]
    core = core.at[:, :RADIUS].add(edges[:, :RADIUS])
    core = core.at[:, tile_height - RADIUS :].add(edges[:, 3 * RADIUS :])
    return (grad_q, core[0].astype(jnp.bfloat16), core[1].astype(jnp.bfloat16))


def solution(mesh):
    placed = (
        P(("lat", "lon"), None, None),
        P(("lat", "lon"), None, None),
        P(("lat", "lon"), None, None),
        P(("lat", "lon"), None, None),
    )
    return jax.shard_map(
        on_device,
        mesh=mesh,
        in_specs=placed,
        out_specs=(P("lat", "lon", None), P("lat", "lon", None), P("lat", "lon", None)),
        check_vma=False,
    )
```

profile of v0, /device:TPU:25, one launch (start us, length us, event | category | flops | bytes accessed | tf_op | source)
XLA Modules:
  0.0 582.8 jit_solution(4372896458404556037)
XLA Ops:
  29.3 9.0 %all-to-all-done.1 = bf16[16,2,8192]{2,1,0:T(2,128)(2,1)S(1)} async-done(((bf16[16,2,8192]{2,1,0:T(2,128)(2,1)}), bf16[16,2,8192]{2,1,0:T(2,128)(2,1)S(1)}, u32[]{:S(2)}, u32[]{:S(2)}) %all-to-all-start.1) | async-done | bytes 524320 | tf_op jit(solution)/shard_map/all_to_all | solution.py:115
  74.7 10.4 %all-to-all-done.3 = bf16[16,2,8192]{2,1,0:T(2,128)(2,1)} async-done(((bf16[16,2,8192]{2,1,0:T(2,128)(2,1)}), bf16[16,2,8192]{2,1,0:T(2,128)(2,1)}, u32[]{:S(2)}, u32[]{:S(2)}) %all-to-all-start.3) | async-done | bytes 524320 | tf_op jit(solution)/shard_map/all_to_all | solution.py:116
  100.4 405.5 %while.22 = (s32[]{:T(128)}, bf16[16,16,1024]{2,1,0:T(8,128)(2,1)}, f32[2,32,32,1024]{3,2,1,0:T(8,128)}, bf16[32,32,1024]{2,1,0:T(8,128)(2,1)}, s32[]{:T(128)}, ...) while((s32[]{:T(128)}, bf16[16,16,1024]{2,1,0:T(8,128)(2,1)}, ...), condition=%wide.region_4.5_spmd.clone, body=%wide.region_0.4_spmd.clone.sunk | while | flops 809437312 | bytes 232929664 | solution.py:108
  150.0 13.8 %fusion.87 = (f32[2,16,8,8]{3,2,1,0:T(8,128)S(1)}, f32[2,16,8,8,24,24]{5,3,4,2,1,0:T(8,128)}) fusion(pred[8,8,24,24]{3,1,2,0:T(8,128)(4,1)S(1)} %copy-done.4, bf16[24,2,8,16,64]{4,2,0,3,1:T(8,128)(2,1)S(1)} %copy-done.6, bf16[24,2,8,16,64]{4,2,0,3,1:T(8,128)(2,1)S(1)} %copy-done.7, bf16[24,2,8,16,64]{4,2,0,3,1:T(8,128)(2,1)S(1)} %copy-done.8, ...), kind=kOutput, calls=%fused_computation.9.clone.1 | convolution fusion | flops 161609728 | bytes 7385088 | tf_op jit(solution)/shard_map/while/body/eval_jaxpr/acbhe,icjhe->chabij/dot_general | solution.py:66
  163.8 14.1 %fusion.88 = f32[2,16,8,8]{3,2,1,0:T(8,128)S(1)} fusion(f32[2,16,8,8,24,24]{5,3,4,2,1,0:T(8,128)} %get-tuple-element.423, f32[2,16,8,8]{3,2,1,0:T(8,128)S(1)} %get-tuple-element.424, pred[8,8,24,24]{3,1,2,0:T(8,128)(4,1)S(1)} %copy-done.4), kind=kLoop, calls=%fused_computation.11.clone.1 | loop fusion | flops 4716544 | bytes 4771840 | tf_op jit(solution)/shard_map/while/body/eval_jaxpr/reduce_sum | solution.py:72
  178.0 21.7 %multiply_reduce_fusion.2 = (f32[2,16,8,8]{3,2,1,0:T(8,128)S(1)}, f32[2,16,8,8,24,24]{5,3,4,2,1,0:T(8,128)}) fusion(f32[2,16,8,8]{3,2,1,0:T(8,128)S(1)} %fusion.88, f32[2,16,8,8]{3,2,1,0:T(8,128)S(1)} %get-tuple-element.424, f32[2,16,8,8,24,24]{5,3,4,2,1,0:T(8,128)} %get-tuple-element.423, pred[8,8,24,24]{3,1,2,0:T(8,128)(4,1)S(1)} %copy-done.4, ...), kind=kOutput, calls=%fused_computation.2.clone.1 | convolution fusion | flops 165148672 | bytes 12120064 | tf_op jit(solution)/shard_map/while/body/eval_jaxpr/acbhe,icjhe->chabij/dot_general | solution.py:74
  199.7 25.8 %fusion.90 = (bf16[2,16,8,8,24,24]{5,3,4,2,1,0:T(8,128)(2,1)}, bf16[2,16,8,8,24,24]{5,3,4,2,1,0:T(8,128)(2,1)}) fusion(f32[2,16,8,8]{3,2,1,0:T(8,128)S(1)} %fusion.88, f32[2,16,8,8]{3,2,1,0:T(8,128)S(1)} %get-tuple-element.424, f32[2,16,8,8,24,24]{5,3,4,2,1,0:T(8,128)} %get-tuple-element.423, pred[8,8,24,24]{3,1,2,0:T(8,128)(4,1)S(1)} %copy-done.4, ...), kind=kLoop, calls=%fused_computation.52.clone.1 | loop fusion | flops 10616832 | bytes 14217216 | tf_op jit(solution)/shard_map/while/body/eval_jaxpr/convert_element_type | solution.py:73
  225.5 10.2 %fusion.91 = bf16[8,2,8,16,64]{4,2,0,3,1:T(8,128)(2,1)S(1)} fusion(bf16[2,16,8,8,24,24]{5,3,4,2,1,0:T(8,128)(2,1)} %get-tuple-element.432, bf16[24,2,8,16,64]{4,2,0,3,1:T(8,128)(2,1)S(1)} %copy-done.6, bf16[24,2,8,16,64]{4,2,0,3,1:T(8,128)(2,1)} %copy.159, bf16[24,2,8,16,64]{4,2,0,3,1:T(8,128)(2,1)} %copy.160), kind=kOutput, calls=%fused_computation.37.clone.1 | convolution fusion | flops 158203904 | bytes 4980736 | tf_op jit(solution)/shard_map/while/body/eval_jaxpr/chabij,icjhe->acbhe/dot_general | solution.py:79
  261.4 13.2 %pad_add_fusion.2 = f32[2,24,4,8,16,64]{5,3,1,4,2,0:T(8,128)} fusion(f32[2,24,2,8,16,64]{5,3,1,4,2,0:T(8,128)} %get-tuple-element.434, f32[2,24,2,8,16,64]{5,3,1,4,2,0:T(8,128)} %get-tuple-element.435, f32[2,24,2,8,16,64]{5,3,1,4,2,0:T(8,128)} %get-tuple-element.436), kind=kLoop, calls=%fused_computation.16.clone.1 | loop fusion | flops 3145728 | bytes 15728640 | tf_op jit(solution)/shard_map/while/body/eval_jaxpr/add | solution.py:98
  274.6 16.4 %copy.165 = f32[2,24,4,8,16,64]{5,4,3,2,1,0:T(8,128)} copy(f32[2,24,4,8,16,64]{5,3,1,4,2,0:T(8,128)} %pad_add_fusion.2) | data formatting | bytes 12582912 | tf_op jit(solution)/shard_map/while/body/eval_jaxpr/add | solution.py:98
  291.0 11.6 %reshape.304 = f32[2,24,32,1024]{3,2,1,0:T(8,128)} reshape(f32[2,24,4,8,16,64]{5,4,3,2,1,0:T(8,128)} %copy.165) | data formatting | bytes 12582912 | tf_op jit(solution)/shard_map/while/body/eval_jaxpr/reshape | solution.py:99
  302.6 9.6 %add_dynamic-update-slice_fusion.2 = f32[2,32,32,1024]{3,2,1,0:T(8,128)} fusion(f32[2,32,32,1024]{3,2,1,0:T(8,128)} %get-tuple-element.453, s32[]{:T(128)S(6)} %select_n.64, f32[2,24,32,1024]{3,2,1,0:T(8,128)} %reshape.304), kind=kLoop, calls=%fused_computation.23.clone.1 | loop fusion | flops 1572864 | bytes 18874372 | tf_op jit(solution)/shard_map/while/body/eval_jaxpr/dynamic_update_slice | solution.py:101
  338.1 13.8 %fusion.87 = (f32[2,16,8,8]{3,2,1,0:T(8,128)S(1)}, f32[2,16,8,8,24,24]{5,3,4,2,1,0:T(8,128)}) fusion(pred[8,8,24,24]{3,1,2,0:T(8,128)(4,1)S(1)} %copy-done.4, bf16[24,2,8,16,64]{4,2,0,3,1:T(8,128)(2,1)S(1)} %copy-done.6, bf16[24,2,8,16,64]{4,2,0,3,1:T(8,128)(2,1)S(1)} %copy-done.7, bf16[24,2,8,16,64]{4,2,0,3,1:T(8,128)(2,1)S(1)} %copy-done.8, ...), kind=kOutput, calls=%fused_computation.9.clone.1 | convolution fusion | flops 161609728 | bytes 7385088 | tf_op jit(solution)/shard_map/while/body/eval_jaxpr/acbhe,icjhe->chabij/dot_general | solution.py:66
  351.9 14.1 %fusion.88 = f32[2,16,8,8]{3,2,1,0:T(8,128)S(1)} fusion(f32[2,16,8,8,24,24]{5,3,4,2,1,0:T(8,128)} %get-tuple-element.423, f32[2,16,8,8]{3,2,1,0:T(8,128)S(1)} %get-tuple-element.424, pred[8,8,24,24]{3,1,2,0:T(8,128)(4,1)S(1)} %copy-done.4), kind=kLoop, calls=%fused_computation.11.clone.1 | loop fusion | flops 4716544 | bytes 4771840 | tf_op jit(solution)/shard_map/while/body/eval_jaxpr/reduce_sum | solution.py:72
  366.0 21.7 %multiply_reduce_fusion.2 = (f32[2,16,8,8]{3,2,1,0:T(8,128)S(1)}, f32[2,16,8,8,24,24]{5,3,4,2,1,0:T(8,128)}) fusion(f32[2,16,8,8]{3,2,1,0:T(8,128)S(1)} %fusion.88, f32[2,16,8,8]{3,2,1,0:T(8,128)S(1)} %get-tuple-element.424, f32[2,16,8,8,24,24]{5,3,4,2,1,0:T(8,128)} %get-tuple-element.423, pred[8,8,24,24]{3,1,2,0:T(8,128)(4,1)S(1)} %copy-done.4, ...), kind=kOutput, calls=%fused_computation.2.clone.1 | convolution fusion | flops 165148672 | bytes 12120064 | tf_op jit(solution)/shard_map/while/body/eval_jaxpr/acbhe,icjhe->chabij/dot_general | solution.py:74
  387.7 25.8 %fusion.90 = (bf16[2,16,8,8,24,24]{5,3,4,2,1,0:T(8,128)(2,1)}, bf16[2,16,8,8,24,24]{5,3,4,2,1,0:T(8,128)(2,1)}) fusion(f32[2,16,8,8]{3,2,1,0:T(8,128)S(1)} %fusion.88, f32[2,16,8,8]{3,2,1,0:T(8,128)S(1)} %get-tuple-element.424, f32[2,16,8,8,24,24]{5,3,4,2,1,0:T(8,128)} %get-tuple-element.423, pred[8,8,24,24]{3,1,2,0:T(8,128)(4,1)S(1)} %copy-done.4, ...), kind=kLoop, calls=%fused_computation.52.clone.1 | loop fusion | flops 10616832 | bytes 14217216 | tf_op jit(solution)/shard_map/while/body/eval_jaxpr/convert_element_type | solution.py:73
  413.5 10.2 %fusion.91 = bf16[8,2,8,16,64]{4,2,0,3,1:T(8,128)(2,1)S(1)} fusion(bf16[2,16,8,8,24,24]{5,3,4,2,1,0:T(8,128)(2,1)} %get-tuple-element.432, bf16[24,2,8,16,64]{4,2,0,3,1:T(8,128)(2,1)S(1)} %copy-done.6, bf16[24,2,8,16,64]{4,2,0,3,1:T(8,128)(2,1)} %copy.159, bf16[24,2,8,16,64]{4,2,0,3,1:T(8,128)(2,1)} %copy.160), kind=kOutput, calls=%fused_computation.37.clone.1 | convolution fusion | flops 158203904 | bytes 4980736 | tf_op jit(solution)/shard_map/while/body/eval_jaxpr/chabij,icjhe->acbhe/dot_general | solution.py:79
  449.4 13.2 %pad_add_fusion.2 = f32[2,24,4,8,16,64]{5,3,1,4,2,0:T(8,128)} fusion(f32[2,24,2,8,16,64]{5,3,1,4,2,0:T(8,128)} %get-tuple-element.434, f32[2,24,2,8,16,64]{5,3,1,4,2,0:T(8,128)} %get-tuple-element.435, f32[2,24,2,8,16,64]{5,3,1,4,2,0:T(8,128)} %get-tuple-element.436), kind=kLoop, calls=%fused_computation.16.clone.1 | loop fusion | flops 3145728 | bytes 15728640 | tf_op jit(solution)/shard_map/while/body/eval_jaxpr/add | solution.py:98
  462.6 16.4 %copy.165 = f32[2,24,4,8,16,64]{5,4,3,2,1,0:T(8,128)} copy(f32[2,24,4,8,16,64]{5,3,1,4,2,0:T(8,128)} %pad_add_fusion.2) | data formatting | bytes 12582912 | tf_op jit(solution)/shard_map/while/body/eval_jaxpr/add | solution.py:98
  479.0 11.6 %reshape.304 = f32[2,24,32,1024]{3,2,1,0:T(8,128)} reshape(f32[2,24,4,8,16,64]{5,4,3,2,1,0:T(8,128)} %copy.165) | data formatting | bytes 12582912 | tf_op jit(solution)/shard_map/while/body/eval_jaxpr/reshape | solution.py:99
  490.6 9.6 %add_dynamic-update-slice_fusion.2 = f32[2,32,32,1024]{3,2,1,0:T(8,128)} fusion(f32[2,32,32,1024]{3,2,1,0:T(8,128)} %get-tuple-element.453, s32[]{:T(128)S(6)} %select_n.64, f32[2,24,32,1024]{3,2,1,0:T(8,128)} %reshape.304), kind=kLoop, calls=%fused_computation.23.clone.1 | loop fusion | flops 1572864 | bytes 18874372 | tf_op jit(solution)/shard_map/while/body/eval_jaxpr/dynamic_update_slice | solution.py:101
  516.3 12.8 %collective-permute-done.5 = bf16[2,28,6,1024]{3,0,2,1:T(2,128)(2,1)S(1)} collective-permute-done((bf16[2,28,6,1024]{3,0,2,1:T(2,128)(2,1)S(1)}, bf16[2,28,6,1024]{3,0,2,1:T(2,128)(2,1)S(1)}, u32[]{:S(2)}, u32[]{:S(2)}) %collective-permute-start.5) | collective-permute-done | bytes 688160 | tf_op jit(solution)/shard_map/ppermute | solution.py:24
  532.4 11.3 %scatter-add.14 = f32[2,28,16,1024]{3,2,1,0:T(8,128)} dynamic-update-slice(f32[2,28,16,1024]{3,2,1,0:T(8,128)} %slice.282, f32[2,28,6,1024]{3,2,1,0:T(8,128)} %convert_add_fusion, s32[]{:T(128)} %constant.215.clone.1, s32[]{:T(128)} %constant.215.clone.1, s32[]{:T(128)} %constant.215.clone.1, s32[]{:T(128)} %constant.215.clone.1) | dynamic-update-slice | bytes 2752516 | tf_op jit(solution)/shard_map/scatter-add | solution.py:133
  547.1 10.4 %scatter-add.15 = f32[2,28,16,1024]{3,2,1,0:T(8,128)} dynamic-update-slice(f32[2,28,16,1024]{3,2,1,0:T(8,128)} %scatter-add.14, f32[2,28,6,1024]{3,2,1,0:T(8,128)} %slice_add_fusion, s32[]{:T(128)} %constant.215.clone.1, s32[]{:T(128)} %constant.215.clone.1, s32[]{:T(128)} %constant.223.clone.1, s32[]{:T(128)} %constant.215.clone.1) | dynamic-update-slice | bytes 2752516 | tf_op jit(solution)/shard_map/scatter-add | solution.py:134
  (193 shorter events, 225.0 us)
Async XLA Ops:
  0.6 13.7 %copy-start.14 = (bf16[1,256,1024]{2,1,0:T(8,128)(2,1)S(1)}, bf16[1,256,1024]{2,1,0:T(8,128)(2,1)}, u32[]{:S(2)}) copy-start(bf16[1,256,1024]{2,1,0:T(8,128)(2,1)} %param.16) | copy-start | bytes 1572868
  8.0 16.0 %all-to-all-start = ((bf16[16,2,8192]{2,1,0:T(2,128)(2,1)}), bf16[16,2,8192]{2,1,0:T(2,128)(2,1)S(1)}, u32[]{:S(2)}, u32[]{:S(2)}) async-start(bf16[16,2,8192]{2,1,0:T(2,128)(2,1)} %reshape.289), calls=%async_computation | async-start | bytes 1048576 | tf_op jit(solution)/shard_map/all_to_all | solution.py:114
  23.9 14.4 %all-to-all-start.1 = ((bf16[16,2,8192]{2,1,0:T(2,128)(2,1)}), bf16[16,2,8192]{2,1,0:T(2,128)(2,1)S(1)}, u32[]{:S(2)}, u32[]{:S(2)}) async-start(bf16[16,2,8192]{2,1,0:T(2,128)(2,1)} %reshape.287), calls=%async_computation.1 | async-start | bytes 1048576 | tf_op jit(solution)/shard_map/all_to_all | solution.py:115
  40.0 15.0 %collective-permute-start = (bf16[2,6,16,1024]{3,2,1,0:T(8,128)(2,1)}, bf16[2,6,16,1024]{3,2,1,0:T(8,128)(2,1)S(1)}, u32[]{:S(2)}, u32[]{:S(2)}) collective-permute-start(bf16[2,6,16,1024]{3,2,1,0:T(8,128)(2,1)} %get-tuple-element.342), channel_id=1, source_target_pairs={{0,16},{16,32},{32,48},{48,64},{64,80},{80,96},{96,112},{112,0},{1... | collective-permute-start | bytes 1179656 | tf_op jit(solution)/shard_map/ppermute | solution.py:21
  42.9 13.1 %collective-permute-start.1 = (bf16[2,6,16,1024]{3,2,1,0:T(8,128)(2,1)}, bf16[2,6,16,1024]{3,2,1,0:T(8,128)(2,1)S(1)}, u32[]{:S(2)}, u32[]{:S(2)}) collective-permute-start(bf16[2,6,16,1024]{3,2,1,0:T(8,128)(2,1)} %get-tuple-element.343), channel_id=1, source_target_pairs={{16,0},{32,16},{48,32},{64,48},{80,64},{96,80},{112,96},{0,112},{1... | collective-permute-start | bytes 1179656 | tf_op jit(solution)/shard_map/ppermute | solution.py:24
  49.9 18.5 %all-to-all-start.2 = ((bf16[16,2,8192]{2,1,0:T(2,128)(2,1)}), bf16[16,2,8192]{2,1,0:T(2,128)(2,1)S(1)}, u32[]{:S(2)}, u32[]{:S(2)}) async-start(bf16[16,2,8192]{2,1,0:T(2,128)(2,1)} %reshape.291), calls=%async_computation.2 | async-start | bytes 1048576 | tf_op jit(solution)/shard_map/all_to_all | solution.py:113
  58.1 30.2 %collective-permute-start.3 = (bf16[2,28,6,1024]{3,0,2,1:T(2,128)(2,1)}, bf16[2,28,6,1024]{3,0,2,1:T(2,128)(2,1)}, u32[]{:S(2)}, u32[]{:S(2)}) collective-permute-start(bf16[2,28,6,1024]{3,0,2,1:T(2,128)(2,1)} %copy.72), channel_id=1, source_target_pairs={{1,0},{2,1},{3,2},{4,3},{5,4},{6,5},{7,6},{8,7},{9,8},{10,9},{11,1... | collective-permute-start | bytes 2064392 | tf_op jit(solution)/shard_map/ppermute | solution.py:24
  62.2 27.4 %collective-permute-start.2 = (bf16[2,28,6,1024]{3,0,2,1:T(2,128)(2,1)}, bf16[2,28,6,1024]{3,0,2,1:T(2,128)(2,1)}, u32[]{:S(2)}, u32[]{:S(2)}) collective-permute-start(bf16[2,28,6,1024]{3,0,2,1:T(2,128)(2,1)} %copy.71), channel_id=1, source_target_pairs={{0,1},{1,2},{2,3},{3,4},{4,5},{5,6},{6,7},{7,8},{8,9},{9,10},{10,1... | collective-permute-start | bytes 2064392 | tf_op jit(solution)/shard_map/ppermute | solution.py:21
  68.4 16.7 %all-to-all-start.3 = ((bf16[16,2,8192]{2,1,0:T(2,128)(2,1)}), bf16[16,2,8192]{2,1,0:T(2,128)(2,1)}, u32[]{:S(2)}, u32[]{:S(2)}) async-start(bf16[16,2,8192]{2,1,0:T(2,128)(2,1)} %reshape.293), calls=%async_computation.3 | async-start | bytes 1048576 | tf_op jit(solution)/shard_map/all_to_all | solution.py:116
  74.5 16.4 %copy-start.13 = (bf16[2,6,16,1024]{3,2,1,0:T(8,128)(2,1)S(1)}, bf16[2,6,16,1024]{3,2,1,0:T(8,128)(2,1)}, u32[]{:S(2)}) copy-start(bf16[2,6,16,1024]{3,2,1,0:T(8,128)(2,1)} %copy-done.12) | copy-start | bytes 1179652
  124.1 12.2 %copy-start.16 = (pred[8,24]{1,0:T(8,128)(4,1)}, pred[8,24]{1,0:T(8,128)(4,1)S(1)}, u32[]{:S(2)}) copy-start(pred[8,24]{1,0:T(8,128)(4,1)S(1)} %get-tuple-element.473) | copy-start | bytes 580 | tf_op jit(solution)/shard_map/while
  163.8 14.1 %copy-start.1 = (bf16[8,2,8,16,64]{4,3,2,1,0:T(8,128)(2,1)S(1)}, bf16[8,2,8,16,64]{4,3,2,1,0:T(8,128)(2,1)}, u32[]{:S(2)}) copy-start(bf16[8,2,8,16,64]{4,3,2,1,0:T(8,128)(2,1)} %reshape.303) | copy-start | bytes 786436 | tf_op jit(solution)/shard_map/while
  302.6 9.6 %copy-start.3 = (bf16[32,32,1024]{2,1,0:T(8,128)(2,1)S(1)}, bf16[32,32,1024]{2,1,0:T(8,128)(2,1)}, u32[]{:S(2)}) copy-start(bf16[32,32,1024]{2,1,0:T(8,128)(2,1)} %copy-done.2) | copy-start | bytes 6291460 | tf_op jit(solution)/shard_map/while
  302.6 9.6 %copy-start.11 = (bf16[16,16,1024]{2,1,0:T(8,128)(2,1)S(1)}, bf16[16,16,1024]{2,1,0:T(8,128)(2,1)}, u32[]{:S(2)}) copy-start(bf16[16,16,1024]{2,1,0:T(8,128)(2,1)} %copy-done.10) | copy-start | bytes 1572868 | tf_op jit(solution)/shard_map/while
  302.6 9.6 %copy-start.17 = (pred[8,24]{1,0:T(8,128)(4,1)S(1)}, pred[8,24]{1,0:T(8,128)(4,1)}, u32[]{:S(2)}) copy-start(pred[8,24]{1,0:T(8,128)(4,1)} %copy-done.16) | copy-start | bytes 580 | tf_op jit(solution)/shard_map/while
  312.2 12.2 %copy-start.16 = (pred[8,24]{1,0:T(8,128)(4,1)}, pred[8,24]{1,0:T(8,128)(4,1)S(1)}, u32[]{:S(2)}) copy-start(pred[8,24]{1,0:T(8,128)(4,1)S(1)} %get-tuple-element.473) | copy-start | bytes 580 | tf_op jit(solution)/shard_map/while
  351.9 14.1 %copy-start.1 = (bf16[8,2,8,16,64]{4,3,2,1,0:T(8,128)(2,1)S(1)}, bf16[8,2,8,16,64]{4,3,2,1,0:T(8,128)(2,1)}, u32[]{:S(2)}) copy-start(bf16[8,2,8,16,64]{4,3,2,1,0:T(8,128)(2,1)} %reshape.303) | copy-start | bytes 786436 | tf_op jit(solution)/shard_map/while
  490.6 9.6 %copy-start.11 = (bf16[16,16,1024]{2,1,0:T(8,128)(2,1)S(1)}, bf16[16,16,1024]{2,1,0:T(8,128)(2,1)}, u32[]{:S(2)}) copy-start(bf16[16,16,1024]{2,1,0:T(8,128)(2,1)} %copy-done.10) | copy-start | bytes 1572868 | tf_op jit(solution)/shard_map/while
  490.6 9.6 %copy-start.17 = (pred[8,24]{1,0:T(8,128)(4,1)S(1)}, pred[8,24]{1,0:T(8,128)(4,1)}, u32[]{:S(2)}) copy-start(pred[8,24]{1,0:T(8,128)(4,1)} %copy-done.16) | copy-start | bytes 580 | tf_op jit(solution)/shard_map/while
  511.2 17.8 %collective-permute-start.5 = (bf16[2,28,6,1024]{3,0,2,1:T(2,128)(2,1)S(1)}, bf16[2,28,6,1024]{3,0,2,1:T(2,128)(2,1)S(1)}, u32[]{:S(2)}, u32[]{:S(2)}) collective-permute-start(bf16[2,28,6,1024]{3,0,2,1:T(2,128)(2,1)S(1)} %copy.78), channel_id=1, source_target_pairs={{1,0},{2,1},{3,2},{4,3},{5,4},{6,5},{7,6},{8,7},{9,8},{10,9},{11,1... | collective-permute-start | bytes 2064392 | tf_op jit(solution)/shard_map/ppermute | solution.py:24
  512.4 16.9 %collective-permute-start.4 = (bf16[2,28,6,1024]{3,0,2,1:T(2,128)(2,1)S(1)}, bf16[2,28,6,1024]{3,0,2,1:T(2,128)(2,1)S(1)}, u32[]{:S(2)}, u32[]{:S(2)}) collective-permute-start(bf16[2,28,6,1024]{3,0,2,1:T(2,128)(2,1)S(1)} %copy.77), channel_id=1, source_target_pairs={{0,1},{1,2},{2,3},{3,4},{4,5},{5,6},{6,7},{7,8},{8,9},{9,10},{10,1... | collective-permute-start | bytes 2064392 | tf_op jit(solution)/shard_map/ppermute | solution.py:21
  557.4 11.2 %copy-start.5 = (f32[2,28,16,1024]{3,2,1,0:T(8,128)S(1)}, f32[2,28,16,1024]{3,2,1,0:T(8,128)}, u32[]{:S(2)}) copy-start(f32[2,28,16,1024]{3,2,1,0:T(8,128)} %scatter-add.15) | copy-start | bytes 11010052
  560.0 13.3 %collective-permute-start.6 = (bf16[2,6,16,1024]{3,2,1,0:T(8,128)(2,1)S(1)}, bf16[2,6,16,1024]{3,2,1,0:T(8,128)(2,1)S(1)}, u32[]{:S(2)}, u32[]{:S(2)}) collective-permute-start(bf16[2,6,16,1024]{3,2,1,0:T(8,128)(2,1)S(1)} %get-tuple-element.336), channel_id=1, source_target_pairs={{0,16},{16,32},{32,48},{48,64},{64,80},{80,96},{96,112},{1,17},{17... | collective-permute-start | bytes 1179656 | tf_op jit(solution)/shard_map/ppermute | solution.py:21
  566.7 14.3 %collective-permute-start.7 = (bf16[2,6,16,1024]{3,2,1,0:T(8,128)(2,1)S(1)}, bf16[2,6,16,1024]{3,2,1,0:T(8,128)(2,1)S(1)}, u32[]{:S(2)}, u32[]{:S(2)}) collective-permute-start(bf16[2,6,16,1024]{3,2,1,0:T(8,128)(2,1)S(1)} %get-tuple-element.337), channel_id=1, source_target_pairs={{16,0},{32,16},{48,32},{64,48},{80,64},{96,80},{112,96},{17,1},{33... | collective-permute-start | bytes 1179656 | tf_op jit(solution)/shard_map/ppermute | solution.py:24
  (26 other events, 140.8 us)
where the time goes:
time: 593 us; the launch traced here: 583 us
  other arithmetic  174 us (29%)
  local copies, waits for them, and re-layouts  165 us (28%)
  matrix products  125 us (21%)
  waiting for transfers between devices  49.5 us (8%)
  starting transfers between devices  38.4 us (6%)
  loops' own time  29.9 us (5%)
    convert_element_type x2, other arithmetic, one_row(): probs_low = probs.astype(jnp.bfloat16)  51.6 us
    dot_general x2, matrix products, one_row(): jnp.einsum('acbhe,icjhe->chabij', d_tile, v_win, preferred_element_type=j...  43.5 us
    add x2, local copies, waits for them, and re-layouts, one_row(): folded = folded + jnp.pad(both[:, :, :, 2], plain + ((2, 0),) + rest)  32.8 us
    another operation x1, loops' own time, window_grads(): return lax.fori_loop(0, tile_rows, one_row, begin)  29.9 us
    reduce_sum x2, other arithmetic, one_row(): probs = weights / jnp.sum(weights, axis=(4, 5), keepdims=True)  28.3 us
    dot_general x2, matrix products, one_row(): jnp.einsum('acbhe,icjhe->chabij', q_tile, k_win, preferred_element_type=j...  27.6 us
    add x2, other arithmetic, one_row(): folded = folded + jnp.pad(both[:, :, :, 2], plain + ((2, 0),) + rest)  26.4 us
    reshape x2, local copies, waits for them, and re-layouts, one_row(): folded = folded.reshape(2, 3 * TILE, query_cols + 2 * TILE, features)  23.2 us
  transfers between devices with their start and end apart: 12, of which 7 were waited for; matrix products, arithmetic and copies ran while one was open for 5% of the time, Pallas kernels for 0%

commit v1 on v0

v1 whole, which is shorter than its diff:
```python
import jax
import jax.numpy as jnp
from jax import lax
from jax.experimental import pallas as pl
from jax.experimental.pallas import tpu as pltpu
from jax.sharding import PartitionSpec as P

RADIUS = 6
SIDE = 8
HEAD = 64
LANES = 128

masked_score = -1e30


def dot(a, b, ca, cb):
    return lax.dot_general(a, b, (((ca,), (cb,)), ((), ())), preferred_element_type=jnp.float32)


def window_mask(lat, lats, half, rows, cols):
    half_rows = rows // 2
    wide = cols + 2 * SIDE
    span = half_rows + 2 * RADIUS
    shape = (span * wide, half_rows * cols)
    key = lax.broadcasted_iota(jnp.int32, shape, 0)
    query = lax.broadcasted_iota(jnp.int32, shape, 1)
    down = key // wide - query // cols
    right = key % wide - query % cols
    row = lat * rows - RADIUS + half * half_rows + key // wide
    ok = (down >= 0) & (down <= 2 * RADIUS)
    ok &= (right >= SIDE - RADIUS) & (right <= SIDE + RADIUS)
    ok &= (row >= 0) & (row < lats * rows)
    ok = jnp.where(ok, 0.0, masked_score)
    return jnp.concatenate([ok, ok], axis=1)


def pair_grads(q, d, k, v, mask):
    lane = lax.broadcasted_iota(jnp.int32, q.shape, 1)
    first = lane < HEAD
    zero = jnp.zeros_like(q)
    q2 = jnp.concatenate([jnp.where(first, q, zero), jnp.where(first, zero, q)], axis=0)
    d2 = jnp.concatenate([jnp.where(first, d, zero), jnp.where(first, zero, d)], axis=0)
    s = dot(k, q2, 1, 1) * (HEAD ** -0.5) + mask
    top = jnp.max(s, axis=0, keepdims=True)
    e = jnp.exp(s - top)
    r = 1.0 / jnp.sum(e, axis=0, keepdims=True)
    p = e * r
    dp = dot(v, d2, 1, 1)
    centre = jnp.sum(p * dp, axis=0, keepdims=True)
    ds = (p * (dp - centre) * (HEAD ** -0.5)).astype(jnp.bfloat16)
    dv = dot(p.astype(jnp.bfloat16), d2, 1, 0)
    dk = dot(ds, q2, 1, 0)
    dq = dot(ds, k, 0, 0)
    count = q.shape[0]
    dq = jnp.where(first, dq[:count], dq[count:])
    return dq, dk, dv


def grads_kernel(lats, lat_ref, own_ref, up_ref, down_ref, dq_ref, mid_ref, upg_ref, downg_ref, mask_ref, total_ref):
    rows, cols = 16, 16
    wide = cols + 2 * SIDE

    @pl.when(pl.program_id(0) == 0)
    def _():
        for half in range(2):
            mask_ref[half] = window_mask(lat_ref[0], lats, half, rows, cols)

    q = own_ref[:, 0:cols, :].reshape(rows * cols, LANES)
    d = own_ref[:, cols:2 * cols, :].reshape(rows * cols, LANES)
    base = 2 * cols

    def keys_of(start):
        parts = [r[:, a + start:a + start + wide, :].reshape(-1, LANES) for r, a in ((up_ref, 0), (own_ref, base), (down_ref, 0))]
        return jnp.concatenate(parts, axis=0)

    k = keys_of(0)
    v = keys_of(wide)
    count = rows * cols // 2
    span = (rows // 2 + 2 * RADIUS) * wide
    shift = (rows // 2) * wide
    for half in range(2):
        here = slice(half * count, (half + 1) * count)
        there = slice(half * shift, half * shift + span)
        dq, dk, dv = pair_grads(q[here], d[here], k[there], v[there], mask_ref[half])
        dq_ref[here, :] = dq.astype(dq_ref.dtype)
        if half == 0:
            total_ref[0, 0:span] = dk
            total_ref[1, 0:span] = dv
        else:
            lap = span - shift
            total_ref[0, shift:span] += dk[:lap]
            total_ref[1, shift:span] += dv[:lap]
            total_ref[0, span:] = dk[lap:]
            total_ref[1, span:] = dv[lap:]
    edge = RADIUS * wide
    total = total_ref[...]
    upg_ref[...] = total[:, :edge].astype(jnp.bfloat16)
    downg_ref[...] = total[:, -edge:].astype(jnp.bfloat16)
    mid_ref[...] = total[:, edge:-edge]


def window_grads(own, up, down, lats):
    rows, cols = 16, 16
    wide = cols + 2 * SIDE
    features = own.shape[-1]
    lat = lax.axis_index("lat").astype(jnp.int32).reshape(1)
    keys = (rows + 2 * RADIUS) * wide
    span = (rows // 2 + 2 * RADIUS) * wide

    def block(shape):
        lead = (0,) * (len(shape) - 1)
        return pl.BlockSpec(shape[:-1] + (LANES,), lambda g: lead + (g,))

    import functools
    outs = [((rows * cols, features), jnp.bfloat16), ((2, rows * wide, features), jnp.float32),
            ((2, RADIUS * wide, features), jnp.bfloat16), ((2, RADIUS * wide, features), jnp.bfloat16)]
    return pl.pallas_call(
        functools.partial(grads_kernel, lats),
        grid=(features // LANES,),
        in_specs=[pl.BlockSpec(memory_space=pltpu.SMEM), block(own.shape), block(up.shape), block(down.shape)],
        out_specs=[block(s) for s, _ in outs],
        out_shape=[jax.ShapeDtypeStruct(s, t) for s, t in outs],
        scratch_shapes=[pltpu.VMEM((2, span, rows * cols), jnp.float32), pltpu.VMEM((2, keys, LANES), jnp.float32)],
        compiler_params=pltpu.CompilerParams(vmem_limit_bytes=48 * 1024 * 1024),
    )(lat, own, up, down)


def on_device(queries, keys, values, grads_out):
    lats, lons = lax.axis_size("lat"), lax.axis_size("lon")
    queries, keys, values, grads_out = (a[0] for a in (queries, keys, values, grads_out))
    features = queries.shape[-1]
    cols = queries.shape[0] // lons
    rows = lons
    wide = cols + 2 * SIDE

    def plain(a):
        return a.reshape(lons, cols, features)

    def extended(a):
        b = plain(a)
        left = jnp.roll(b, 1, axis=0)[:, cols - SIDE:]
        right = jnp.roll(b, -1, axis=0)[:, :SIDE]
        return jnp.concatenate([left, b, right], axis=1)

    chunks = jnp.concatenate([plain(queries), plain(grads_out), extended(keys), extended(values)], axis=1)
    own = lax.all_to_all(chunks, "lon", split_axis=0, concat_axis=0, tiled=True)
    higher = [(i, i + 1) for i in range(lats - 1)]
    lower = [(i + 1, i) for i in range(lats - 1)]
    kv = own[:, 2 * cols:]
    up = lax.ppermute(kv[rows - RADIUS:], "lat", higher)
    down = lax.ppermute(kv[:RADIUS], "lat", lower)
    dq, mid, up_grad, down_grad = window_grads(own, up, down, lats)
    from_low = lax.ppermute(down_grad, "lat", higher)
    from_high = lax.ppermute(up_grad, "lat", lower)
    f32 = jnp.float32
    edge = RADIUS * wide
    mid = jnp.concatenate([mid[:, :edge] + from_low.astype(f32), mid[:, edge:-edge], mid[:, -edge:] + from_high.astype(f32)], axis=1)
    mid = mid.reshape(2, rows, wide, features)
    right = [(i, (i + 1) % lons) for i in range(lons)]
    left = [((i + 1) % lons, i) for i in range(lons)]
    from_left = lax.ppermute(mid[:, :, wide - SIDE:].astype(jnp.bfloat16), "lon", right)
    from_right = lax.ppermute(mid[:, :, :SIDE].astype(jnp.bfloat16), "lon", left)
    core = mid[:, :, SIDE:SIDE + cols] + jnp.concatenate([from_left, from_right], axis=2).astype(f32)
    core = core.astype(jnp.bfloat16)
    return dq.reshape(rows, cols, features), core[0], core[1]


def solution(mesh):
    placed = P(("lat", "lon"), None, None)
    return jax.shard_map(
        on_device,
        mesh=mesh,
        in_specs=(placed,) * 4,
        out_specs=(P("lat", "lon", None),) * 3,
        check_vma=False,
    )
```

time: 593 us -> 147 us (0.25); the launches traced: 583 us -> 146 us
  other arithmetic: 174 us -> 3.85 us
  local copies, waits for them, and re-layouts: 165 us -> 7.74 us
  matrix products: 125 us -> 0 us
  blocking collectives: 0 us -> 43.9 us
  loops' own time: 29.9 us -> 0 us
  Pallas kernels: 0 us -> 17.2 us
  starting transfers between devices: 38.4 us -> 28.3 us
    dot_general x10 -> x0, matrix products: 125 us -> none  [the longest x2 43.5 us: one_row(): jnp.einsum('acbhe,icjhe->chabij', d_tile, v_win, preferred_element_type=j...]
    convert_element_type x2 -> x1, other arithmetic: 51.6 us -> 0.44 us  [on_device(): core = core.astype(jnp.bfloat16)]
    reshape x10 -> x0, local copies, waits for them, and re-layouts: 44.3 us -> none  [the longest x2 23.2 us: one_row(): folded = folded.reshape(2, 3 * TILE, query_cols + 2 * TILE, features)]
    all_to_all x0 -> x1, blocking collectives: none -> 43.9 us  [on_device(): own = lax.all_to_all(chunks, 'lon', split_axis=0, concat_axis=0, tiled=True)]
    add x2 -> x0, local copies, waits for them, and re-layouts: 32.8 us -> none  [one_row(): folded = folded + jnp.pad(both[:, :, :, 2], plain + ((2, 0),) + rest)]
    another operation x1 -> x0, loops' own time: 29.9 us -> none  [window_grads(): return lax.fori_loop(0, tile_rows, one_row, begin)]
    add x4 -> x1, other arithmetic: 31.8 us -> 2.43 us  [on_device(): mid[:, :edge] + from_low.astype(f32)]
    reduce_sum x2 -> x0, other arithmetic: 28.3 us -> none  [one_row(): probs = weights / jnp.sum(weights, axis=(4, 5), keepdims=True)]
  transfers between devices with their start and end apart: 12 -> 6, of which waited for: 7 -> 5; matrix products, arithmetic and copies ran while one was open for 5% -> 1% of each run, Pallas kernels for 0% -> 0%
where the time goes in v1:
time: 147 us; the launch traced here: 146 us
  waiting for transfers between devices  44 us (30%)
  blocking collectives  43.9 us (30%)
  starting transfers between devices  28.3 us (19%)
  Pallas kernels  17.2 us (12%)
  local copies, waits for them, and re-layouts  7.74 us (5%)
  other arithmetic  3.85 us (3%)
    all_to_all x1, blocking collectives, on_device(): own = lax.all_to_all(chunks, 'lon', split_axis=0, concat_axis=0, tiled=True)  43.9 us
    pallas_call x1, Pallas kernels, window_grads(): pl.pallas_call(functools.partial(grads_kernel, lats), grid=(features // L...  17.2 us
    ppermute x1, waiting for transfers between devices, on_device(): down = lax.ppermute(kv[:RADIUS], 'lat', lower)  14.3 us
    ppermute x1, waiting for transfers between devices, on_device(): from_low = lax.ppermute(down_grad, 'lat', higher)  11.1 us
    ppermute x1, waiting for transfers between devices, on_device(): lax.ppermute(mid[:, :, wide - SIDE:].astype(jnp.bfloat16), 'lon', right)  10.3 us
    ppermute x1, starting transfers between devices, on_device(): lax.ppermute(mid[:, :, wide - SIDE:].astype(jnp.bfloat16), 'lon', right)  9.8 us
    ppermute x1, starting transfers between devices, on_device(): from_low = lax.ppermute(down_grad, 'lat', higher)  7.71 us
    ppermute x1, waiting for transfers between devices, on_device(): from_high = lax.ppermute(up_grad, 'lat', lower)  7.45 us
  transfers between devices with their start and end apart: 6, of which 5 were waited for; matrix products, arithmetic and copies ran while one was open for 1% of the time, Pallas kernels for 0%

profile of v1, /device:TPU:25, one launch (start us, length us, event | category | flops | bytes accessed | tf_op | source)
XLA Modules:
  0.0 145.8 jit_solution(1842473635423264001)
XLA Ops:
  0.6 0.9 fusion.10
  1.5 1.3 fusion.9
  2.8 0.8 fusion.8
  3.6 1.3 fusion.7
  5.2 0.8 copy-done.2
  6.0 43.9 %all_to_all.5.own_ref = bf16[16,96,1024]{2,1,0:T(8,128)(2,1)S(1)} all-to-all(bf16[16,96,1024]{2,1,0:T(8,128)(2,1)S(1)} %fusion.1), channel_id=1, replica_groups=mesh['lat'=8,'lon'=16] {'lon'}, dimensions={0} | all-to-all | bytes 6291456 | tf_op jit(solution)/shard_map/all_to_all | solution.py:146
  49.9 0.1 fusion.5
  50.0 2.4 %collective-permute-start.1 = (bf16[6,64,1024]{2,1,0:T(8,128)(2,1)S(1)}, bf16[6,64,1024]{2,1,0:T(8,128)(2,1)S(1)}, u32[]{:S(2)}, u32[]{:S(2)}) collective-permute-start(bf16[6,64,1024]{2,1,0:T(8,128)(2,1)S(1)} %get-tuple-element.13), channel_id=1, source_target_pairs={{16,0},{32,16},{48,32},{64,48},{80,64},{96,80},{112,96},{17,1},{33... | collective-permute-start | bytes 2359304 | tf_op jit(solution)/shard_map/ppermute | solution.py:151
  52.4 6.5 %collective-permute-start = (bf16[6,64,1024]{2,1,0:T(8,128)(2,1)S(1)}, bf16[6,64,1024]{2,1,0:T(8,128)(2,1)S(1)}, u32[]{:S(2)}, u32[]{:S(2)}) collective-permute-start(bf16[6,64,1024]{2,1,0:T(8,128)(2,1)S(1)} %get-tuple-element.14), channel_id=1, source_target_pairs={{0,16},{16,32},{32,48},{48,64},{64,80},{80,96},{96,112},{1,17},{17... | collective-permute-start | bytes 2359304 | tf_op jit(solution)/shard_map/ppermute | solution.py:150
  58.9 14.3 %collective-permute-done.1.down_ref = bf16[6,64,1024]{2,1,0:T(8,128)(2,1)S(1)} collective-permute-done((bf16[6,64,1024]{2,1,0:T(8,128)(2,1)S(1)}, bf16[6,64,1024]{2,1,0:T(8,128)(2,1)S(1)}, u32[]{:S(2)}, u32[]{:S(2)}) %collective-permute-start.1) | collective-permute-done | bytes 786464 | tf_op jit(solution)/shard_map/ppermute | solution.py:151
  73.2 0.9 collective-permute-done.up_ref
  74.1 17.2 %shard_map.67 = (bf16[256,1024]{1,0:T(8,128)(2,1)}, f32[2,512,1024]{2,1,0:T(8,128)}, bf16[2,192,1024]{2,1,0:T(8,128)(2,1)S(1)}, bf16[2,192,1024]{2,1,0:T(8,128)(2,1)S(1)}) custom-call(s32[1]{0:T(128)} %bitcast.lat_ref, bf16[16,96,1024]{2,1,0:T(8,128)(2,1)} %copy-done, bf16[6,64,1024]{2,1,0:T(8,128)(2,1)S(1)} %collective-permute-done.up_ref, ...), custom_call_target="tpu_custom_call" | custom-call | tf_op jit(solution)/shard_map/pallas_call | solution.py:117
  91.3 7.7 %collective-permute-start.2 = (bf16[2,192,1024]{2,1,0:T(8,128)(2,1)S(1)}, bf16[2,192,1024]{2,1,0:T(8,128)(2,1)S(1)}, u32[]{:S(2)}, u32[]{:S(2)}) collective-permute-start(bf16[2,192,1024]{2,1,0:T(8,128)(2,1)S(1)} %get-tuple-element.9), channel_id=1, source_target_pairs={{0,16},{16,32},{32,48},{48,64},{64,80},{80,96},{96,112},{1,17},{17... | collective-permute-start | bytes 2359304 | tf_op jit(solution)/shard_map/ppermute | solution.py:153
  99.1 1.9 %collective-permute-start.3 = (bf16[2,192,1024]{2,1,0:T(8,128)(2,1)S(1)}, bf16[2,192,1024]{2,1,0:T(8,128)(2,1)S(1)}, u32[]{:S(2)}, u32[]{:S(2)}) collective-permute-start(bf16[2,192,1024]{2,1,0:T(8,128)(2,1)S(1)} %get-tuple-element.10), channel_id=1, source_target_pairs={{16,0},{32,16},{48,32},{64,48},{80,64},{96,80},{112,96},{17,1},{33... | collective-permute-start | bytes 2359304 | tf_op jit(solution)/shard_map/ppermute | solution.py:154
  101.0 1.3 slice.110
  102.3 11.1 %collective-permute-done.2 = bf16[2,192,1024]{2,1,0:T(8,128)(2,1)S(1)} collective-permute-done((bf16[2,192,1024]{2,1,0:T(8,128)(2,1)S(1)}, bf16[2,192,1024]{2,1,0:T(8,128)(2,1)S(1)}, u32[]{:S(2)}, u32[]{:S(2)}) %collective-permute-start.2) | collective-permute-done | bytes 786464 | tf_op jit(solution)/shard_map/ppermute | solution.py:153
  113.4 7.5 %collective-permute-done.3 = bf16[2,192,1024]{2,1,0:T(8,128)(2,1)S(1)} collective-permute-done((bf16[2,192,1024]{2,1,0:T(8,128)(2,1)S(1)}, bf16[2,192,1024]{2,1,0:T(8,128)(2,1)S(1)}, u32[]{:S(2)}, u32[]{:S(2)}) %collective-permute-start.3) | collective-permute-done | bytes 786464 | tf_op jit(solution)/shard_map/ppermute | solution.py:154
  120.8 2.4 %convert_add_fusion.1 = (f32[2,192,1024]{2,1,0:T(8,128)S(1)}, f32[2,192,1024]{2,1,0:T(8,128)S(1)}) fusion(bf16[2,192,1024]{2,1,0:T(8,128)(2,1)S(1)} %collective-permute-done.2, f32[2,512,1024]{2,1,0:T(8,128)} %get-tuple-element.8, bf16[2,192,1024]{2,1,0:T(8,128)(2,1)S(1)} %collective-permute-done.3), kind=kLoop, calls=%fused_computation.4 | loop fusion | flops 1572864 | bytes 7864320 | tf_op jit(solution)/shard_map/add | solution.py:157
  123.2 0.6 pad_maximum_fusion
  123.8 0.3 convert.4
  124.2 9.8 %collective-permute-start.4 = (bf16[2,16,8,1024]{3,2,1,0:T(8,128)(2,1)S(1)}, bf16[2,16,8,1024]{3,2,1,0:T(8,128)(2,1)S(1)}, u32[]{:S(2)}, u32[]{:S(2)}) collective-permute-start(bf16[2,16,8,1024]{3,2,1,0:T(8,128)(2,1)S(1)} %get-tuple-element.15), channel_id=1, source_target_pairs={{0,1},{1,2},{2,3},{3,4},{4,5},{5,6},{6,7},{7,8},{8,9},{9,10},{10,1... | collective-permute-start | bytes 1572872 | tf_op jit(solution)/shard_map/ppermute | solution.py:161
  134.1 10.3 %collective-permute-done.4 = bf16[2,16,8,1024]{3,2,1,0:T(8,128)(2,1)S(1)} collective-permute-done((bf16[2,16,8,1024]{3,2,1,0:T(8,128)(2,1)S(1)}, bf16[2,16,8,1024]{3,2,1,0:T(8,128)(2,1)S(1)}, u32[]{:S(2)}, u32[]{:S(2)}) %collective-permute-start.4) | collective-permute-done | bytes 524320 | tf_op jit(solution)/shard_map/ppermute | solution.py:161
  144.3 0.4 fusion
  144.8 1.0 slice_bitcast_fusion
  (20 shorter events, 0.3 us)
Async XLA Ops:
  0.6 4.3 %copy-start.3 = (bf16[1,256,1024]{2,1,0:T(8,128)(2,1)S(1)}, bf16[1,256,1024]{2,1,0:T(8,128)(2,1)}, u32[]{:S(2)}) copy-start(bf16[1,256,1024]{2,1,0:T(8,128)(2,1)} %param.4) | copy-start | bytes 1572868
  0.6 4.3 %copy-start.4 = (bf16[1,256,1024]{2,1,0:T(8,128)(2,1)S(1)}, bf16[1,256,1024]{2,1,0:T(8,128)(2,1)}, u32[]{:S(2)}) copy-start(bf16[1,256,1024]{2,1,0:T(8,128)(2,1)} %param.7) | copy-start | bytes 1572868
  1.5 3.5 %copy-start.1 = (bf16[1,256,1024]{2,1,0:T(8,128)(2,1)S(1)}, bf16[1,256,1024]{2,1,0:T(8,128)(2,1)}, u32[]{:S(2)}) copy-start(bf16[1,256,1024]{2,1,0:T(8,128)(2,1)} %param.5) | copy-start | bytes 1572868
  4.9 1.0 copy-start.2
  49.9 2.5 %copy-start = (bf16[16,96,1024]{2,1,0:T(8,128)(2,1)}, bf16[16,96,1024]{2,1,0:T(8,128)(2,1)S(1)}, u32[]{:S(2)}) copy-start(bf16[16,96,1024]{2,1,0:T(8,128)(2,1)S(1)} %all_to_all.5.own_ref) | copy-start | bytes 9437188
  50.0 23.2 %collective-permute-start.1 = (bf16[6,64,1024]{2,1,0:T(8,128)(2,1)S(1)}, bf16[6,64,1024]{2,1,0:T(8,128)(2,1)S(1)}, u32[]{:S(2)}, u32[]{:S(2)}) collective-permute-start(bf16[6,64,1024]{2,1,0:T(8,128)(2,1)S(1)} %get-tuple-element.13), channel_id=1, source_target_pairs={{16,0},{32,16},{48,32},{64,48},{80,64},{96,80},{112,96},{17,1},{33... | collective-permute-start | bytes 2359304 | tf_op jit(solution)/shard_map/ppermute | solution.py:151
  52.4 21.7 %collective-permute-start = (bf16[6,64,1024]{2,1,0:T(8,128)(2,1)S(1)}, bf16[6,64,1024]{2,1,0:T(8,128)(2,1)S(1)}, u32[]{:S(2)}, u32[]{:S(2)}) collective-permute-start(bf16[6,64,1024]{2,1,0:T(8,128)(2,1)S(1)} %get-tuple-element.14), channel_id=1, source_target_pairs={{0,16},{16,32},{32,48},{48,64},{64,80},{80,96},{96,112},{1,17},{17... | collective-permute-start | bytes 2359304 | tf_op jit(solution)/shard_map/ppermute | solution.py:150
  91.3 22.0 %collective-permute-start.2 = (bf16[2,192,1024]{2,1,0:T(8,128)(2,1)S(1)}, bf16[2,192,1024]{2,1,0:T(8,128)(2,1)S(1)}, u32[]{:S(2)}, u32[]{:S(2)}) collective-permute-start(bf16[2,192,1024]{2,1,0:T(8,128)(2,1)S(1)} %get-tuple-element.9), channel_id=1, source_target_pairs={{0,16},{16,32},{32,48},{48,64},{64,80},{80,96},{96,112},{1,17},{17... | collective-permute-start | bytes 2359304 | tf_op jit(solution)/shard_map/ppermute | solution.py:153
  99.1 21.7 %collective-permute-start.3 = (bf16[2,192,1024]{2,1,0:T(8,128)(2,1)S(1)}, bf16[2,192,1024]{2,1,0:T(8,128)(2,1)S(1)}, u32[]{:S(2)}, u32[]{:S(2)}) collective-permute-start(bf16[2,192,1024]{2,1,0:T(8,128)(2,1)S(1)} %get-tuple-element.10), channel_id=1, source_target_pairs={{16,0},{32,16},{48,32},{64,48},{80,64},{96,80},{112,96},{17,1},{33... | collective-permute-start | bytes 2359304 | tf_op jit(solution)/shard_map/ppermute | solution.py:154
  124.2 20.1 %collective-permute-start.4 = (bf16[2,16,8,1024]{3,2,1,0:T(8,128)(2,1)S(1)}, bf16[2,16,8,1024]{3,2,1,0:T(8,128)(2,1)S(1)}, u32[]{:S(2)}, u32[]{:S(2)}) collective-permute-start(bf16[2,16,8,1024]{3,2,1,0:T(8,128)(2,1)S(1)} %get-tuple-element.15), channel_id=1, source_target_pairs={{0,1},{1,2},{2,3},{3,4},{4,5},{5,6},{6,7},{7,8},{8,9},{9,10},{10,1... | collective-permute-start | bytes 1572872 | tf_op jit(solution)/shard_map/ppermute | solution.py:161
  134.1 10.3 %collective-permute-start.5 = (bf16[2,16,8,1024]{3,2,1,0:T(8,128)(2,1)S(1)}, bf16[2,16,8,1024]{3,2,1,0:T(8,128)(2,1)S(1)}, u32[]{:S(2)}, u32[]{:S(2)}) collective-permute-start(bf16[2,16,8,1024]{3,2,1,0:T(8,128)(2,1)S(1)} %get-tuple-element.16), channel_id=1, source_target_pairs={{1,0},{2,1},{3,2},{4,3},{5,4},{6,5},{7,6},{8,7},{9,8},{10,9},{11,1... | collective-permute-start | bytes 1572872 | tf_op jit(solution)/shard_map/ppermute | solution.py:162

commit v2 on v1

v2 whole, which is shorter than its diff:
```python
import functools
import itertools

import jax
import jax.numpy as jnp
from jax import lax
from jax.experimental import pallas as pl
from jax.experimental.pallas import tpu as pltpu
from jax.sharding import PartitionSpec as P

HEAD = 64
LANES = 128
RADIUS = 6
SIDE = 8
ROWS = 16
TILE = 16
COLS = 2 * TILE
WIDE = COLS + 2 * SIDE
TALL = ROWS + 2 * RADIUS
HALF = ROWS // 2
SPAN = HALF + 2 * RADIUS
TWIDE = TILE + 2 * SIDE
BLOCKS = 4
CHIPS = 8
SPREAD = 15

MESH = pl.DeviceIdType.MESH
bf16 = jnp.bfloat16
f32 = jnp.float32
masked_score = -1e30


def dot(a, b, ca, cb):
    return lax.dot_general(a, b, (((ca,), (cb,)), ((), ())), preferred_element_type=f32)


def window_mask(lat, lats, half):
    shape = (SPAN * TWIDE, HALF * TILE)
    key = lax.broadcasted_iota(jnp.int32, shape, 0)
    query = lax.broadcasted_iota(jnp.int32, shape, 1)
    down = key // TWIDE - query // TILE
    right = key % TWIDE - query % TILE
    row = lat * ROWS - RADIUS + half * HALF + key // TWIDE
    ok = (down >= 0) & (down <= 2 * RADIUS)
    ok &= (right >= SIDE - RADIUS) & (right <= SIDE + RADIUS)
    ok &= (row >= 0) & (row < lats * ROWS)
    ok = jnp.where(ok, 0.0, masked_score)
    return jnp.concatenate([ok, ok], axis=1)


def pair_grads(q, d, k, v, mask):
    first = lax.broadcasted_iota(jnp.int32, q.shape, 1) < HEAD
    zero = jnp.zeros_like(q)
    q = q * (HEAD ** -0.5)
    q2 = jnp.concatenate([jnp.where(first, q, zero), jnp.where(first, zero, q)], axis=0)
    d2 = jnp.concatenate([jnp.where(first, d, zero), jnp.where(first, zero, d)], axis=0)
    s = dot(k, q2, 1, 1) + mask
    e = jnp.exp(s - jnp.max(s, axis=0, keepdims=True))
    p = e * (1.0 / jnp.sum(e, axis=0, keepdims=True))
    dp = dot(v, d2, 1, 1)
    centre = jnp.sum(p * dp, axis=0, keepdims=True)
    ds = (p * (dp - centre)).astype(bf16)
    dv = dot(p.astype(bf16), d2, 1, 0)
    dk = dot(ds, q2, 1, 0)
    dq = dot(ds, k, 0, 0) * (HEAD ** -0.5)
    count = q.shape[0]
    return jnp.where(first, dq[:count], dq[count:]), dk, dv


STEPS = [(1, 0, 0), (3, 0, 0), (0, 1, 0), (2, 0, 0), (1, 1, 0), (3, 1, 0), (0, 1, 1), (2, 1, 0), (1, 0, 1),
         (3, 0, 1), (2, 0, 1), (1, 1, 1), (3, 1, 1), (2, 1, 1), (0, 0, 1)]


def kernel(lats, q_ref, k_ref, v_ref, d_ref, out_ref, send_kv, send_qd, got_kv, got_qd, mask, acc, edge_out, edge_in,
           side_out, side_in, final, sent_kv, sent_qd, came_kv, came_qd, own_sem, relay_out, relay_in, lat_out, lat_in,
           lon_out, lon_in, swap_out, swap_in, keep_sem):
    lat, lon = lax.axis_index("lat"), lax.axis_index("lon")
    x, z, core = lon // 4, (lon // 2) % 2, lon % 2
    chip = lon // 2
    partner = (lat, 2 * chip + 1 - core)
    left = (lat, 2 * ((chip + CHIPS - 1) % CHIPS) + core)
    right = (lat, 2 * ((chip + 1) % CHIPS) + core)
    above, below = (lat - 1, lon), (lat + 1, lon)
    has_above, has_below = lat > 0, lat < lats - 1

    def other(step):
        return lat, (((x + step[0]) % 4) * 2 + (z + step[1]) % 2) * 2 + (core + step[2]) % 2

    barrier = pltpu.get_barrier_semaphore()
    for step in STEPS:
        pl.semaphore_signal(barrier, inc=1, device_id=other(step), device_id_type=MESH)

    @pl.when(has_above)
    def _():
        pl.semaphore_signal(barrier, inc=1, device_id=above, device_id_type=MESH)

    @pl.when(has_below)
    def _():
        pl.semaphore_signal(barrier, inc=1, device_id=below, device_id_type=MESH)

    def prepare(b):
        for c in range(2):
            lanes = pl.ds(pl.multiple_of(c * BLOCKS * LANES + b * LANES, LANES), LANES)
            for i, ref in enumerate((k_ref, v_ref)):
                a = ref[0, :, lanes].astype(f32)
                a = jnp.concatenate([a[-SIDE:], a, a[:SIDE]], axis=0).astype(bf16)
                for m in range(CHIPS):
                    send_kv[b, 2 * m + c, i * WIDE:(i + 1) * WIDE] = a[m * COLS:m * COLS + WIDE]
            for i, ref in enumerate((q_ref, d_ref)):
                for m in range(CHIPS):
                    send_qd[b, 2 * m + c, i * COLS:(i + 1) * COLS] = ref[0, m * COLS:(m + 1) * COLS, lanes]

    def spread(b):
        for out, into, gone, came, row, i in ((send_kv, got_kv, sent_kv, came_kv, lon + RADIUS, 0),
                                              (send_qd, got_qd, sent_qd, came_qd, lon, 1)):
            for step in STEPS:
                to = other(step)
                pltpu.make_async_remote_copy(out.at[b, to[1]], into.at[b, row], gone.at[b], came.at[b],
                                             device_id=to, device_id_type=MESH).start()
            pltpu.make_async_copy(out.at[b, lon], into.at[b, row], own_sem.at[b, i]).start()

    def own_wait(b, out, into, row, i):
        pltpu.make_async_copy(out.at[b, lon], into.at[b, row], own_sem.at[b, i]).wait()

    def all_wait(ref, sem, b):
        pltpu.make_async_copy(ref.at[b, 0:SPREAD], ref.at[b, 0:SPREAD], sem.at[b]).wait()

    prepare(0)
    peers = SPREAD + (lat + lats - 1) // lats + (2 * lats - 2 - lat) // lats
    pl.semaphore_wait(barrier, peers)

    @pl.loop(0, BLOCKS)
    def _(b):
        spread(b)

        @pl.when(b < BLOCKS - 1)
        def _():
            prepare(b + 1)

    for half in range(2):
        mask[half] = window_mask(lat, lats, half)

    @pl.when(lat == 0)
    def _():
        for b in range(BLOCKS):
            got_kv[b, 0:RADIUS] = jnp.zeros((RADIUS, 2 * WIDE, LANES), bf16)

    @pl.when(lat == lats - 1)
    def _():
        for b in range(BLOCKS):
            got_kv[b, TALL - RADIUS:TALL] = jnp.zeros((RADIUS, 2 * WIDE, LANES), bf16)

    def relay_up(b):
        return pltpu.make_async_remote_copy(got_kv.at[b, RADIUS:2 * RADIUS], got_kv.at[b, TALL - RADIUS:TALL], relay_out.at[b, 0],
                                            relay_in.at[b, 0], device_id=above, device_id_type=MESH)

    def relay_down(b):
        return pltpu.make_async_remote_copy(got_kv.at[b, ROWS:ROWS + RADIUS], got_kv.at[b, 0:RADIUS], relay_out.at[b, 1],
                                            relay_in.at[b, 1], device_id=below, device_id_type=MESH)

    def edge_up(b):
        return pltpu.make_async_remote_copy(edge_out.at[b, 0], edge_in.at[b, 0], lat_out.at[b, 0], lat_in.at[b, 0],
                                            device_id=above, device_id_type=MESH)

    def edge_down(b):
        return pltpu.make_async_remote_copy(edge_out.at[b, 1], edge_in.at[b, 1], lat_out.at[b, 1], lat_in.at[b, 1],
                                            device_id=below, device_id_type=MESH)

    def side_left(b):
        return pltpu.make_async_remote_copy(side_out.at[b, 0], side_in.at[b, 0], lon_out.at[b, 0], lon_in.at[b, 0],
                                            device_id=left, device_id_type=MESH)

    def side_right(b):
        return pltpu.make_async_remote_copy(side_out.at[b, 1], side_in.at[b, 1], lon_out.at[b, 1], lon_in.at[b, 1],
                                            device_id=right, device_id_type=MESH)

    out_lanes = lambda b: pl.ds(pl.multiple_of(core * BLOCKS * LANES + b * LANES, LANES), LANES)

    def swap(b):
        return pltpu.make_async_remote_copy(final.at[b, 1 - core], out_ref.at[:, :, :, out_lanes(b)], swap_out.at[b], swap_in.at[b],
                                            device_id=partner, device_id_type=MESH)

    def keep(b):
        return pltpu.make_async_copy(final.at[b, core], out_ref.at[:, :, :, out_lanes(b)], keep_sem.at[b])

    def pass_keys(b):
        own_wait(b, send_kv, got_kv, lon + RADIUS, 0)
        all_wait(got_kv, came_kv, b)

        @pl.when(has_above)
        def _():
            relay_up(b).start()

        @pl.when(has_below)
        def _():
            relay_down(b).start()

    def compute(b):
        own_wait(b, send_qd, got_qd, lon, 1)
        all_wait(got_qd, came_qd, b)
        acc[b] = jnp.zeros((2, TALL, WIDE, LANES), f32)

        def tiles(half):
            @pl.loop(0, 2)
            def _(t):
                rows = slice(half * HALF, (half + 1) * HALF)
                spans = slice(half * HALF, half * HALF + SPAN)
                at = lambda start, size: pl.ds(pl.multiple_of(start + t * TILE, TILE), size)
                q = got_qd[b, rows, at(0, TILE)].reshape(HALF * TILE, LANES)
                d = got_qd[b, rows, at(COLS, TILE)].reshape(HALF * TILE, LANES)
                k = got_kv[b, spans, at(0, TWIDE)].reshape(SPAN * TWIDE, LANES)
                v = got_kv[b, spans, at(WIDE, TWIDE)].reshape(SPAN * TWIDE, LANES)
                dq, dk, dv = pair_grads(q, d, k, v, mask[half])
                final[b, t, 0, rows] = dq.astype(bf16).reshape(HALF, TILE, LANES)
                acc[b, 0, spans, at(0, TWIDE)] += dk.reshape(SPAN, TWIDE, LANES)
                acc[b, 1, spans, at(0, TWIDE)] += dv.reshape(SPAN, TWIDE, LANES)

        @pl.when(has_above)
        def _():
            relay_down(b).wait_recv()

        tiles(0)

        @pl.when(has_above)
        def _():
            edge_out[b, 0] = acc[b, :, 0:RADIUS].astype(bf16)
            edge_up(b).start()

        @pl.when(has_below)
        def _():
            relay_up(b).wait_recv()

        tiles(1)

        @pl.when(has_below)
        def _():
            edge_out[b, 1] = acc[b, :, TALL - RADIUS:TALL].astype(bf16)
            edge_down(b).start()

    def add_edges(b):
        @pl.when(has_below)
        def _():
            edge_up(b).wait_recv()
            acc[b, :, ROWS:ROWS + RADIUS] += edge_in[b, 0].astype(f32)

        @pl.when(has_above)
        def _():
            edge_down(b).wait_recv()
            acc[b, :, RADIUS:2 * RADIUS] += edge_in[b, 1].astype(f32)

        own = slice(RADIUS, RADIUS + ROWS)
        side_out[b, 0] = jnp.concatenate([acc[b, 0, own, 0:SIDE], acc[b, 1, own, 0:SIDE]], axis=1).astype(bf16)
        side_out[b, 1] = jnp.concatenate([acc[b, 0, own, WIDE - SIDE:WIDE], acc[b, 1, own, WIDE - SIDE:WIDE]], axis=1).astype(bf16)
        side_left(b).start()
        side_right(b).start()

    def add_sides(b):
        own = slice(RADIUS, RADIUS + ROWS)
        side_left(b).wait_recv()
        side_right(b).wait_recv()
        from_right = side_in[b, 0].astype(f32)
        from_left = side_in[b, 1].astype(f32)
        for i in range(2):
            whole = acc[b, i, own, SIDE:SIDE + COLS]
            part = slice(i * SIDE, (i + 1) * SIDE)
            whole = jnp.concatenate([whole[:, :SIDE] + from_left[:, part], whole[:, SIDE:COLS - SIDE],
                                     whole[:, COLS - SIDE:] + from_right[:, part]], axis=1).astype(bf16)
            final[b, 0, 1 + i] = whole[:, :TILE]
            final[b, 1, 1 + i] = whole[:, TILE:]
        swap(b).start()
        keep(b).start()

    @pl.loop(0, BLOCKS + 2)
    def _(i):
        @pl.when(i < BLOCKS)
        def _():
            pass_keys(i)

        @pl.when(i >= 2)
        def _():
            add_sides(i - 2)

        @pl.when((i >= 1) & (i < BLOCKS + 1))
        def _():
            add_edges(i - 1)

        @pl.when(i < BLOCKS)
        def _():
            compute(i)

    @pl.loop(0, BLOCKS)
    def _(b):
        all_wait(got_kv, sent_kv, b)
        all_wait(got_qd, sent_qd, b)
        side_left(b).wait_send()
        side_right(b).wait_send()

        @pl.when(has_above)
        def _():
            relay_up(b).wait_send()
            edge_up(b).wait_send()

        @pl.when(has_below)
        def _():
            relay_down(b).wait_send()
            edge_down(b).wait_send()

        keep(b).wait()
        swap(b).wait()


def on_device(queries, keys, values, grads_out):
    lats = lax.axis_size("lat")
    features = queries.shape[-1]
    vmem = lambda *shape: pltpu.VMEM(shape, bf16)
    sems = lambda *shape: pltpu.SemaphoreType.DMA(shape)
    lons = 2 * CHIPS
    out = pl.pallas_call(
        functools.partial(kernel, lats),
        out_shape=jax.ShapeDtypeStruct((3, ROWS, TILE, features), bf16),
        in_specs=[pl.BlockSpec(memory_space=pltpu.VMEM)] * 4,
        out_specs=pl.BlockSpec(memory_space=pl.ANY),
        scratch_shapes=[
            vmem(BLOCKS, lons, 2 * WIDE, LANES),
            vmem(BLOCKS, lons, 2 * COLS, LANES),
            vmem(BLOCKS, TALL, 2 * WIDE, LANES),
            vmem(BLOCKS, ROWS, 2 * COLS, LANES),
            pltpu.VMEM((2, SPAN * TWIDE, 2 * HALF * TILE), f32),
            pltpu.VMEM((BLOCKS, 2, TALL, WIDE, LANES), f32),
            vmem(BLOCKS, 2, 2, RADIUS, WIDE, LANES),
            vmem(BLOCKS, 2, 2, RADIUS, WIDE, LANES),
            vmem(BLOCKS, 2, ROWS, 2 * SIDE, LANES),
            vmem(BLOCKS, 2, ROWS, 2 * SIDE, LANES),
            vmem(BLOCKS, 2, 3, ROWS, TILE, LANES),
            sems(BLOCKS), sems(BLOCKS), sems(BLOCKS), sems(BLOCKS),
            sems(BLOCKS, 2), sems(BLOCKS, 2), sems(BLOCKS, 2), sems(BLOCKS, 2), sems(BLOCKS, 2),
            sems(BLOCKS, 2), sems(BLOCKS, 2), sems(BLOCKS), sems(BLOCKS), sems(BLOCKS),
        ],
        compiler_params=pltpu.CompilerParams(collective_id=0, has_side_effects=True, vmem_limit_bytes=56 * 1024 * 1024),
    )(queries, keys, values, grads_out)
    return out[0], out[1], out[2]


def solution(mesh):
    placed = P(("lat", "lon"), None, None)
    return jax.shard_map(
        on_device,
        mesh=mesh,
        in_specs=(placed,) * 4,
        out_specs=(P("lat", "lon", None),) * 3,
        check_vma=False,
    )
```

time: 147 us -> 91 us (0.62)
  the two profiles are of different devices: /device:TPU:25 before, /device:TPU:17 now
where the time goes in v2:
time: 91 us; the launch traced here: 90.9 us
  Pallas kernels  87.7 us (96%)
  local copies, waits for them, and re-layouts  2.54 us (3%)
    pallas_call x1, Pallas kernels, on_device(): pl.pallas_call(functools.partial(kernel, lats), out_shape=jax.ShapeDtypeS...  87.7 us
    squeeze x1, local copies, waits for them, and re-layouts, on_device(): return (out[0], out[1], out[2])  2.54 us

profile of v2, /device:TPU:17, one launch (start us, length us, event | category | flops | bytes accessed | tf_op | source)
XLA Modules:
  0.0 90.9 jit_solution(5306562537340099151)
XLA Ops:
  0.6 87.7 %shard_map.67 = bf16[3,16,16,1024]{3,2,1,0:T(8,128)(2,1)} custom-call(bf16[1,256,1024]{2,1,0:T(8,128)(2,1)} %q_ref.1, bf16[1,256,1024]{2,1,0:T(8,128)(2,1)} %k_ref.1, bf16[1,256,1024]{2,1,0:T(8,128)(2,1)} %v_ref.1, bf16[1,256,1024]{2,1,0:T(8,128)(2,1)} %d_ref.1), custom_call_target="tpu_custom_call" | custom-call | tf_op jit(solution)/shard_map/pallas_call | solution.py:318
  88.3 2.5 %slice_bitcast_fusion = (bf16[16,16,1024]{2,1,0:T(8,128)(2,1)}, bf16[16,16,1024]{2,1,0:T(8,128)(2,1)}, bf16[16,16,1024]{2,1,0:T(8,128)(2,1)}) fusion(bf16[3,16,16,1024]{3,2,1,0:T(8,128)(2,1)} %shard_map.67), kind=kLoop, calls=%fused_computation | loop fusion | bytes 3145728 | tf_op jit(solution)/shard_map/squeeze | solution.py:341

commit v3 on v2

v3 whole, which is shorter than its diff:
```python
import functools

import jax
import jax.numpy as jnp
from jax import lax
from jax.experimental import pallas as pl
from jax.experimental.pallas import tpu as pltpu
from jax.sharding import PartitionSpec as P

HEAD = 64
LANES = 128
RADIUS = 6
SIDE = 8
LON = 256
ROWS = 16
TILE = 16
TILES = 8
STAGES = 4
STEP = 2 * TILE
COLS = TILES * TILE
WIDE = COLS + 2 * SIDE
TALL = ROWS + 2 * RADIUS
HALF = ROWS // 2
SPAN = HALF + 2 * RADIUS
TWIDE = TILE + 2 * SIDE
DEVICES = 16
OTHERS = DEVICES - 1

MESH = pl.DeviceIdType.MESH
bf16 = jnp.bfloat16
f32 = jnp.float32
masked_score = -1e30


def dot(a, b, ca, cb):
    return lax.dot_general(a, b, (((ca,), (cb,)), ((), ())), preferred_element_type=f32)


def window_mask(lat, lats, half):
    shape = (SPAN * TWIDE, HALF * TILE)
    key = lax.broadcasted_iota(jnp.int32, shape, 0)
    query = lax.broadcasted_iota(jnp.int32, shape, 1)
    down = key // TWIDE - query // TILE
    right = key % TWIDE - query % TILE
    row = lat * ROWS - RADIUS + half * HALF + key // TWIDE
    ok = (down >= 0) & (down <= 2 * RADIUS)
    ok &= (right >= SIDE - RADIUS) & (right <= SIDE + RADIUS)
    ok &= (row >= 0) & (row < lats * ROWS)
    ok = jnp.where(ok, 0.0, masked_score)
    return jnp.concatenate([ok, ok], axis=1)


def pair_grads(q, d, k, v, mask):
    first = lax.broadcasted_iota(jnp.int32, q.shape, 1) < HEAD
    zero = jnp.zeros_like(q)
    q = q * (HEAD ** -0.5)
    q2 = jnp.concatenate([jnp.where(first, q, zero), jnp.where(first, zero, q)], axis=0)
    d2 = jnp.concatenate([jnp.where(first, d, zero), jnp.where(first, zero, d)], axis=0)
    s = dot(k, q2, 1, 1) + mask
    e = jnp.exp(s - jnp.max(s, axis=0, keepdims=True))
    p = e * (1.0 / jnp.sum(e, axis=0, keepdims=True))
    dp = dot(v, d2, 1, 1)
    centre = jnp.sum(p * dp, axis=0, keepdims=True)
    ds = (p * (dp - centre)).astype(bf16)
    dv = dot(p.astype(bf16), d2, 1, 0)
    dk = dot(ds, q2, 1, 0)
    dq = dot(ds, k, 0, 0) * (HEAD ** -0.5)
    count = q.shape[0]
    return jnp.where(first, dq[:count], dq[count:]), dk, dv


HOPS = [(1, 0, 0), (3, 0, 0), (0, 1, 0), (2, 0, 0), (1, 1, 0), (3, 1, 0), (0, 1, 1), (2, 1, 0), (1, 0, 1),
        (3, 0, 1), (2, 0, 1), (1, 1, 1), (3, 1, 1), (2, 1, 1), (0, 0, 1)]


def either(core, a, b):
    return (1 - core) * a + core * b


def by(value, unit):
    return pl.multiple_of(value, unit)


def kernel(lats, q_ref, k_ref, v_ref, d_ref, out_ref, raw, shifted, send_qd, got_kv, got_qd, mask, acc, edge_out, edge_in,
           last_out, last_in, side_out, side_in, final_q, final_kv, load_sem, sent_kv, sent_qd, came_kv, came_qd, own_sem,
           relay_out, relay_in, lat_out, lat_in, side_gone, side_came, q_gone, q_came, kv_gone, kv_came):
    lat, lon = lax.axis_index("lat"), lax.axis_index("lon")
    x, z, core = lon // 4, (lon // 2) % 2, lon % 2
    deep = lats // 2
    group = 2 * x + (z + lat // deep) % 2
    partner = (lat, lon + 1 - 2 * core)
    has_above, has_below = lat > 0, lat < lats - 1
    more_above, more_below = (lat + lats - 1) // lats, (2 * lats - 2 - lat) // lats

    def neighbour(other_lat):
        return other_lat, 4 * x + 2 * ((z + lat // deep + other_lat // deep) % 2) + core

    above, below = neighbour(lat - more_above), neighbour(lat + more_below)

    def start_block(g, c):
        return (2 * g + (DEVICES // 2) * c) % DEVICES

    def other(hop):
        ox, oz, oc = (x + hop[0]) % 4, (z + hop[1]) % 2, (core + hop[2]) % 2
        return 4 * ox + 2 * oz + oc, 2 * ox + (oz + lat // deep) % 2, oc

    loads = [pltpu.make_async_copy(r.at[0], t, load_sem.at[i]) for i, (r, t) in enumerate(
        ((k_ref, raw.at[0]), (v_ref, raw.at[1]), (q_ref, send_qd.at[0]), (d_ref, send_qd.at[1])))]
    for load in loads:
        load.start()

    barrier = pltpu.get_barrier_semaphore()
    for hop in HOPS:
        pl.semaphore_signal(barrier, inc=1, device_id=(lat, other(hop)[0]), device_id_type=MESH)

    @pl.when(has_above)
    def _():
        pl.semaphore_signal(barrier, inc=1, device_id=above, device_id_type=MESH)

    @pl.when(has_below)
    def _():
        pl.semaphore_signal(barrier, inc=1, device_id=below, device_id_type=MESH)

    def kv_at(u, c):
        return either(c, 16 + STEP * u, 96 - STEP * u)

    def q_at(u, c):
        return either(c, STEP * u, 96 - STEP * u)

    def done_at(u):
        return by(either(core, STEP * u, 112 - STEP * u), TILE)

    def tile_of(i):
        return either(core, i, TILES - 1 - i)

    for i in range(2):
        loads[i].wait()
        for g in range(8):
            lanes = slice(g * LANES, (g + 1) * LANES)
            a = raw[i, :, lanes].astype(f32)
            a = jnp.concatenate([a[-SIDE:], a, a[:STEP - SIDE]], axis=0)
            shifted[i, :, lanes] = a.astype(bf16)
    loads[2].wait()
    loads[3].wait()

    pl.semaphore_wait(barrier, OTHERS + more_above + more_below)

    def kv_copy(u, g, c, first):
        off = either(c, 0, 96) if first else kv_at(u, c)
        size = 3 * TILE if first else STEP
        begin = (TILE * start_block(g, c) + off) % LON
        src = shifted.at[:, pl.ds(by(begin, TILE), size), pl.ds(by(g * LANES, LANES), LANES)]
        return src, got_kv.at[:, lon + RADIUS, pl.ds(by(off, TILE), size), :]

    def qd_copy(u, g, c):
        off = q_at(u, c)
        begin = (TILE * start_block(g, c) + off) % LON
        src = send_qd.at[:, pl.ds(by(begin, TILE), STEP), pl.ds(by(g * LANES, LANES), LANES)]
        return src, got_qd.at[:, lon, pl.ds(by(off, TILE), STEP), :]

    def spread(u, first=False):
        for kind in range(2):
            gone, came = ((sent_kv, came_kv), (sent_qd, came_qd))[kind]
            for hop in HOPS:
                to, g, c = other(hop)
                src, dst = qd_copy(u, g, c) if kind else kv_copy(u, g, c, first)
                pltpu.make_async_remote_copy(src, dst, gone.at[u], came.at[u], device_id=(lat, to), device_id_type=MESH).start()
            src, dst = qd_copy(u, group, core) if kind else kv_copy(u, group, core, first)
            pltpu.make_async_copy(src, dst, own_sem.at[u, kind]).start()

    spread(0, True)

    @pl.loop(1, STAGES)
    def _(u):
        spread(u)

    for half in range(2):
        mask[half] = window_mask(lat, lats, half)

    @pl.loop(0, TALL)
    def _(row):
        acc[:, row] = jnp.zeros((2, WIDE, LANES), f32)

    @pl.when(lat == 0)
    def _():
        got_kv[:, 0:RADIUS] = jnp.zeros((2, RADIUS, WIDE, LANES), bf16)

    @pl.when(lat == lats - 1)
    def _():
        got_kv[:, TALL - RADIUS:TALL] = jnp.zeros((2, RADIUS, WIDE, LANES), bf16)

    def came_wait(sem, u, ref, size):
        blank = ref.at[:, 0:OTHERS, 0:size, :]
        pltpu.make_async_copy(blank, blank, sem.at[u]).wait()

    def own_wait(u, kind, ref, size):
        blank = ref.at[:, 0, 0:size, :]
        pltpu.make_async_copy(blank, blank, own_sem.at[u, kind]).wait()

    def relay(u, way, first):
        off = either(core, 0, 96) if first else kv_at(u, core)
        cols = pl.ds(by(off, TILE), 3 * TILE if first else STEP)
        here, there, to = ((slice(RADIUS, 2 * RADIUS), slice(TALL - RADIUS, TALL), above),
                           (slice(ROWS, ROWS + RADIUS), slice(0, RADIUS), below))[way]
        return pltpu.make_async_remote_copy(got_kv.at[:, here, cols, :], got_kv.at[:, there, cols, :], relay_out.at[u, way],
                                            relay_in.at[u, way], device_id=to, device_id_type=MESH)

    def edge(u, way):
        return pltpu.make_async_remote_copy(edge_out.at[u, way], edge_in.at[u, way], lat_out.at[u, way], lat_in.at[u, way],
                                            device_id=(above, below)[way], device_id_type=MESH)

    def last_edge(way):
        return pltpu.make_async_remote_copy(last_out.at[way], last_in.at[way], lat_out.at[STAGES, way], lat_in.at[STAGES, way],
                                            device_id=(above, below)[way], device_id_type=MESH)

    def side(i):
        return pltpu.make_async_remote_copy(side_out.at[i], side_in.at[i], side_gone.at[i], side_came.at[i],
                                            device_id=partner, device_id_type=MESH)

    out_lanes = pl.ds(by(group * LANES, LANES), LANES)

    def owner(i):
        return (start_block(group, core) + tile_of(i)) % DEVICES

    def q_pair(i):
        return final_q.at[i], out_ref.at[0, :, :, out_lanes]

    def kv_pair(i):
        return final_kv.at[i], out_ref.at[1:3, :, :, out_lanes]

    def hand_out(pair, i, gone, came):
        src, dst = pair(i)
        to = owner(i)

        @pl.when(to == lon)
        def _():
            pltpu.make_async_copy(src, dst, came.at[group]).start()

        @pl.when(to != lon)
        def _():
            pltpu.make_async_remote_copy(src, dst, gone.at[i], came.at[group], device_id=(lat, to), device_id_type=MESH).start()

    def hand_out_wait(pair, i, gone):
        src, dst = pair(i)
        to = owner(i)

        @pl.when(to != lon)
        def _():
            pltpu.make_async_remote_copy(src, dst, gone.at[i], gone.at[i], device_id=(lat, to), device_id_type=MESH).wait_send()

    own = slice(RADIUS, RADIUS + ROWS)

    def hand_out_kv(i):
        at = pl.ds(by(SIDE + TILE * tile_of(i), SIDE), TILE)
        final_kv[i] = acc[:, own, at].astype(bf16)
        hand_out(kv_pair, i, kv_gone, kv_came)

    def on_ways(make, then):
        @pl.when(has_above)
        def _():
            then(make(0))

        @pl.when(has_below)
        def _():
            then(make(1))

    def pass_keys(u):
        def go(first):
            size = 3 * TILE if first else STEP
            own_wait(u, 0, got_kv, size)
            came_wait(came_kv, u, got_kv, size)
            on_ways(lambda way: relay(u, way, first), lambda copy: copy.start())

        @pl.when(u == 0)
        def _():
            go(True)

        @pl.when(u > 0)
        def _():
            go(False)

    def relay_wait(u, way):
        @pl.when(u == 0)
        def _():
            relay(u, way, True).wait_recv()

        @pl.when(u > 0)
        def _():
            relay(u, way, False).wait_recv()

    def compute(u):
        own_wait(u, 1, got_qd, STEP)
        came_wait(came_qd, u, got_qd, STEP)

        def tiles(half):
            @pl.loop(0, 2)
            def _(j):
                i = 2 * u + j
                begin = by(tile_of(i) * TILE, TILE)
                rows = slice(half * HALF, (half + 1) * HALF)
                spans = slice(half * HALF, half * HALF + SPAN)
                at, near = pl.ds(begin, TILE), pl.ds(begin, TWIDE)
                q = got_qd[0, rows, at].reshape(HALF * TILE, LANES)
                d = got_qd[1, rows, at].reshape(HALF * TILE, LANES)
                k = got_kv[0, spans, near].reshape(SPAN * TWIDE, LANES)
                v = got_kv[1, spans, near].reshape(SPAN * TWIDE, LANES)
                dq, dk, dv = pair_grads(q, d, k, v, mask[half])
                final_q[i, rows] = dq.astype(bf16).reshape(HALF, TILE, LANES)
                acc[0, spans, near] += dk.reshape(SPAN, TWIDE, LANES)
                acc[1, spans, near] += dv.reshape(SPAN, TWIDE, LANES)

        last = by((1 - core) * COLS, TILE)

        def send_edge(way):
            rows = (slice(0, RADIUS), slice(TALL - RADIUS, TALL))[way]
            edge_out[u, way] = acc[:, rows, pl.ds(done_at(u), STEP)].astype(bf16)
            edge(u, way).start()

            @pl.when(u == STAGES - 1)
            def _():
                last_out[way] = acc[:, rows, pl.ds(last, TILE)].astype(bf16)
                last_edge(way).start()

        @pl.when(has_above)
        def _():
            relay_wait(u, 1)

        tiles(0)

        @pl.when(has_above)
        def _():
            send_edge(0)

        @pl.when(has_below)
        def _():
            relay_wait(u, 0)

        tiles(1)

        @pl.when(has_below)
        def _():
            send_edge(1)

        hand_out(q_pair, 2 * u, q_gone, q_came)
        hand_out(q_pair, 2 * u + 1, q_gone, q_came)

    def add_edges(u):
        last = by((1 - core) * COLS, TILE)

        def add(way):
            rows = (slice(ROWS, ROWS + RADIUS), slice(RADIUS, 2 * RADIUS))[way]
            edge(u, way).wait_recv()
            acc[:, rows, pl.ds(done_at(u), STEP)] += edge_in[u, way].astype(f32)

            @pl.when(u == STAGES - 1)
            def _():
                last_edge(way).wait_recv()
                acc[:, rows, pl.ds(last, TILE)] += last_in[way].astype(f32)

        @pl.when(has_below)
        def _():
            add(0)

        @pl.when(has_above)
        def _():
            add(1)

        def send_side(i, at):
            cols = pl.ds(by(at, SIDE), SIDE)
            side_out[i] = jnp.concatenate([acc[0, own, cols], acc[1, own, cols]], axis=1).astype(bf16)
            side(i).start()

        @pl.when(u == 0)
        def _():
            send_side(0, core * (WIDE - SIDE))

        @pl.when(u == STAGES - 1)
        def _():
            send_side(1, (1 - core) * (WIDE - SIDE))

        @pl.when(u > 0)
        def _():
            hand_out_kv(2 * u - 1)
            hand_out_kv(2 * u)

    def add_side(i, at, tile):
        side(i).wait_recv()
        cols = pl.ds(by(at, SIDE), SIDE)
        got = side_in[i].astype(f32)
        acc[0, own, cols] += got[:, :SIDE]
        acc[1, own, cols] += got[:, SIDE:]
        hand_out_kv(tile)

    @pl.loop(0, STAGES + 1)
    def _(i):
        @pl.when(i < STAGES)
        def _():
            pass_keys(i)

        @pl.when(i == 2)
        def _():
            add_side(0, either(core, SIDE, COLS), 0)

        @pl.when(i > 0)
        def _():
            add_edges(i - 1)

        @pl.when(i < STAGES)
        def _():
            compute(i)

    add_side(1, either(core, COLS, SIDE), TILES - 1)

    came_wait(sent_kv, 0, got_kv, 3 * TILE)
    came_wait(sent_qd, 0, got_qd, STEP)
    on_ways(lambda way: relay(0, way, True), lambda copy: copy.wait_send())
    on_ways(lambda way: edge(0, way), lambda copy: copy.wait_send())

    @pl.loop(1, STAGES)
    def _(u):
        came_wait(sent_kv, u, got_kv, STEP)
        came_wait(sent_qd, u, got_qd, STEP)
        on_ways(lambda way: relay(u, way, False), lambda copy: copy.wait_send())
        on_ways(lambda way: edge(u, way), lambda copy: copy.wait_send())

    on_ways(last_edge, lambda copy: copy.wait_send())
    side(0).wait_send()
    side(1).wait_send()

    @pl.loop(0, TILES)
    def _(i):
        hand_out_wait(q_pair, i, q_gone)
        hand_out_wait(kv_pair, i, kv_gone)
        for pair, came in ((q_pair, q_came), (kv_pair, kv_came)):
            src, dst = pair(i)
            pltpu.make_async_copy(src, dst, came.at[i]).wait()


def on_device(queries, keys, values, grads_out):
    lats = lax.axis_size("lat")
    features = queries.shape[-1]
    vmem = lambda *shape: pltpu.VMEM(shape, bf16)
    sems = lambda *shape: pltpu.SemaphoreType.DMA(shape)
    out = pl.pallas_call(
        functools.partial(kernel, lats),
        out_shape=jax.ShapeDtypeStruct((3, ROWS, TILE, features), bf16),
        in_specs=[pl.BlockSpec(memory_space=pl.ANY)] * 4,
        out_specs=pl.BlockSpec(memory_space=pl.ANY),
        scratch_shapes=[
            vmem(2, LON, features),
            vmem(2, LON + STEP, features),
            vmem(2, LON, features),
            vmem(2, TALL, WIDE, LANES),
            vmem(2, ROWS, COLS, LANES),
            pltpu.VMEM((2, SPAN * TWIDE, 2 * HALF * TILE), f32),
            pltpu.VMEM((2, TALL, WIDE, LANES), f32),
            vmem(STAGES, 2, 2, RADIUS, STEP, LANES),
            vmem(STAGES, 2, 2, RADIUS, STEP, LANES),
            vmem(2, 2, RADIUS, TILE, LANES),
            vmem(2, 2, RADIUS, TILE, LANES),
            vmem(2, ROWS, 2 * SIDE, LANES),
            vmem(2, ROWS, 2 * SIDE, LANES),
            vmem(TILES, ROWS, TILE, LANES),
            vmem(TILES, 2, ROWS, TILE, LANES),
            sems(4), sems(STAGES), sems(STAGES), sems(STAGES), sems(STAGES), sems(STAGES, 2),
            sems(STAGES, 2), sems(STAGES, 2), sems(STAGES + 1, 2), sems(STAGES + 1, 2), sems(2), sems(2),
            sems(TILES), sems(TILES), sems(TILES), sems(TILES),
        ],
        compiler_params=pltpu.CompilerParams(collective_id=0, has_side_effects=True, vmem_limit_bytes=56 * 1024 * 1024),
    )(queries, keys, values, grads_out)
    return out[0], out[1], out[2]


def solution(mesh):
    placed = P(("lat", "lon"), None, None)
    return jax.shard_map(
        on_device,
        mesh=mesh,
        in_specs=(placed,) * 4,
        out_specs=(P("lat", "lon", None),) * 3,
        check_vma=False,
    )
```

time: 91 us -> 67.6 us (0.74)
  the two profiles are of different devices: /device:TPU:17 before, /device:TPU:25 now
where the time goes in v3:
time: 67.6 us; the launch traced here: 67 us
  Pallas kernels  63.8 us (94%)
  local copies, waits for them, and re-layouts  2.54 us (4%)
    pallas_call x1, Pallas kernels, on_device(): pl.pallas_call(functools.partial(kernel, lats), out_shape=jax.ShapeDtypeS...  63.8 us
    squeeze x1, local copies, waits for them, and re-layouts, on_device(): return (out[0], out[1], out[2])  2.54 us

profile of v3, /device:TPU:25, one launch (start us, length us, event | category | flops | bytes accessed | tf_op | source)
XLA Modules:
  0.0 67.0 jit_solution(16841239532597593442)
XLA Ops:
  0.6 63.8 %shard_map.67 = bf16[3,16,16,1024]{3,2,1,0:T(8,128)(2,1)} custom-call(bf16[1,256,1024]{2,1,0:T(8,128)(2,1)} %q_ref.1, bf16[1,256,1024]{2,1,0:T(8,128)(2,1)} %k_ref.1, bf16[1,256,1024]{2,1,0:T(8,128)(2,1)} %v_ref.1, bf16[1,256,1024]{2,1,0:T(8,128)(2,1)} %d_ref.1), custom_call_target="tpu_custom_call" | custom-call | tf_op jit(solution)/shard_map/pallas_call | solution.py:444
  64.4 2.5 %slice_bitcast_fusion = (bf16[16,16,1024]{2,1,0:T(8,128)(2,1)}, bf16[16,16,1024]{2,1,0:T(8,128)(2,1)}, bf16[16,16,1024]{2,1,0:T(8,128)(2,1)}) fusion(bf16[3,16,16,1024]{3,2,1,0:T(8,128)(2,1)} %shard_map.67), kind=kLoop, calls=%fused_computation | loop fusion | bytes 3145728 | tf_op jit(solution)/shard_map/squeeze | solution.py:471

commit v4 on v3

--- a/solution.py
+++ b/solution.py
@@ -15,7 +15,7 @@
 ROWS = 16
 TILE = 16
 TILES = 8
-STAGES = 4
+PARTS = 4
 STEP = 2 * TILE
 COLS = TILES * TILE
 WIDE = COLS + 2 * SIDE
@@ -82,7 +82,7 @@
 
 
 def kernel(lats, q_ref, k_ref, v_ref, d_ref, out_ref, raw, shifted, send_qd, got_kv, got_qd, mask, acc, edge_out, edge_in,
-           last_out, last_in, side_out, side_in, final_q, final_kv, load_sem, sent_kv, sent_qd, came_kv, came_qd, own_sem,
+           last_out, last_in, side_out, side_in, final_q, final_kv, load_sem, sent_kv, sent_qd, came_kv, came_qd, own_kv, own_qd,
            relay_out, relay_in, lat_out, lat_in, side_gone, side_came, q_gone, q_came, kv_gone, kv_came):
     lat, lon = lax.axis_index("lat"), lax.axis_index("lon")
     x, z, core = lon // 4, (lon // 2) % 2, lon % 2
@@ -124,14 +124,11 @@
     def kv_at(u, c):
         return either(c, 16 + STEP * u, 96 - STEP * u)
 
-    def q_at(u, c):
-        return either(c, STEP * u, 96 - STEP * u)
-
-    def done_at(u):
-        return by(either(core, STEP * u, 112 - STEP * u), TILE)
-
-    def tile_of(i):
-        return either(core, i, TILES - 1 - i)
+    def done_at(i):
+        return by(either(core, TILE * i, COLS - TILE * i), TILE)
+
+    def tile_of(i, c):
+        return either(c, i, TILES - 1 - i)
 
     for i in range(2):
         loads[i].wait()
@@ -152,27 +149,38 @@
         src = shifted.at[:, pl.ds(by(begin, TILE), size), pl.ds(by(g * LANES, LANES), LANES)]
         return src, got_kv.at[:, lon + RADIUS, pl.ds(by(off, TILE), size), :]
 
-    def qd_copy(u, g, c):
-        off = q_at(u, c)
+    def qd_copy(i, g, c):
+        off = TILE * tile_of(i, c)
         begin = (TILE * start_block(g, c) + off) % LON
-        src = send_qd.at[:, pl.ds(by(begin, TILE), STEP), pl.ds(by(g * LANES, LANES), LANES)]
-        return src, got_qd.at[:, lon, pl.ds(by(off, TILE), STEP), :]
-
-    def spread(u, first=False):
-        for kind in range(2):
-            gone, came = ((sent_kv, came_kv), (sent_qd, came_qd))[kind]
-            for hop in HOPS:
-                to, g, c = other(hop)
-                src, dst = qd_copy(u, g, c) if kind else kv_copy(u, g, c, first)
-                pltpu.make_async_remote_copy(src, dst, gone.at[u], came.at[u], device_id=(lat, to), device_id_type=MESH).start()
-            src, dst = qd_copy(u, group, core) if kind else kv_copy(u, group, core, first)
-            pltpu.make_async_copy(src, dst, own_sem.at[u, kind]).start()
-
-    spread(0, True)
-
-    @pl.loop(1, STAGES)
+        src = send_qd.at[:, pl.ds(by(begin, TILE), TILE), pl.ds(by(g * LANES, LANES), LANES)]
+        return src, got_qd.at[:, lon, pl.ds(by(off, TILE), TILE), :]
+
+    def spread(pair, i, gone, came, own_sem):
+        for hop in HOPS:
+            to, g, c = other(hop)
+            src, dst = pair(i, g, c)
+            pltpu.make_async_remote_copy(src, dst, gone.at[i], came.at[i], device_id=(lat, to), device_id_type=MESH).start()
+        src, dst = pair(i, group, core)
+        pltpu.make_async_copy(src, dst, own_sem.at[i]).start()
+
+    def spread_kv(u, first=False):
+        spread(lambda i, g, c: kv_copy(i, g, c, first), u, sent_kv, came_kv, own_kv)
+
+    def spread_qd(i):
+        spread(qd_copy, i, sent_qd, came_qd, own_qd)
+
+    spread_kv(0, True)
+    spread_qd(0)
+
+    @pl.loop(1, PARTS)
     def _(u):
-        spread(u)
+        spread_kv(u)
+
+        @pl.loop(2 * u - 1, 2 * u + 1)
+        def _(i):
+            spread_qd(i)
+
+    spread_qd(TILES - 1)
 
     for half in range(2):
         mask[half] = window_mask(lat, lats, half)
@@ -193,9 +201,9 @@
         blank = ref.at[:, 0:OTHERS, 0:size, :]
         pltpu.make_async_copy(blank, blank, sem.at[u]).wait()
 
-    def own_wait(u, kind, ref, size):
+    def own_wait(sem, u, ref, size):
         blank = ref.at[:, 0, 0:size, :]
-        pltpu.make_async_copy(blank, blank, own_sem.at[u, kind]).wait()
+        pltpu.make_async_copy(blank, blank, sem.at[u]).wait()
 
     def relay(u, way, first):
         off = either(core, 0, 96) if first else kv_at(u, core)
@@ -210,7 +218,7 @@
                                             device_id=(above, below)[way], device_id_type=MESH)
 
     def last_edge(way):
-        return pltpu.make_async_remote_copy(last_out.at[way], last_in.at[way], lat_out.at[STAGES, way], lat_in.at[STAGES, way],
+        return pltpu.make_async_remote_copy(last_out.at[way], last_in.at[way], lat_out.at[TILES, way], lat_in.at[TILES, way],
                                             device_id=(above, below)[way], device_id_type=MESH)
 
     def side(i):
@@ -220,7 +228,7 @@
     out_lanes = pl.ds(by(group * LANES, LANES), LANES)
 
     def owner(i):
-        return (start_block(group, core) + tile_of(i)) % DEVICES
+        return (start_block(group, core) + tile_of(i, core)) % DEVICES
 
     def q_pair(i):
         return final_q.at[i], out_ref.at[0, :, :, out_lanes]
@@ -250,10 +258,9 @@
 
     own = slice(RADIUS, RADIUS + ROWS)
 
-    def hand_out_kv(i):
-        at = pl.ds(by(SIDE + TILE * tile_of(i), SIDE), TILE)
+    def finish_kv(i):
+        at = pl.ds(by(SIDE + TILE * tile_of(i, core), SIDE), TILE)
         final_kv[i] = acc[:, own, at].astype(bf16)
-        hand_out(kv_pair, i, kv_gone, kv_came)
 
     def on_ways(make, then):
         @pl.when(has_above)
@@ -267,7 +274,7 @@
     def pass_keys(u):
         def go(first):
             size = 3 * TILE if first else STEP
-            own_wait(u, 0, got_kv, size)
+            own_wait(own_kv, u, got_kv, size)
             came_wait(came_kv, u, got_kv, size)
             on_ways(lambda way: relay(u, way, first), lambda copy: copy.start())
 
@@ -288,71 +295,61 @@
         def _():
             relay(u, way, False).wait_recv()
 
-    def compute(u):
-        own_wait(u, 1, got_qd, STEP)
-        came_wait(came_qd, u, got_qd, STEP)
-
-        def tiles(half):
-            @pl.loop(0, 2)
-            def _(j):
-                i = 2 * u + j
-                begin = by(tile_of(i) * TILE, TILE)
-                rows = slice(half * HALF, (half + 1) * HALF)
-                spans = slice(half * HALF, half * HALF + SPAN)
-                at, near = pl.ds(begin, TILE), pl.ds(begin, TWIDE)
-                q = got_qd[0, rows, at].reshape(HALF * TILE, LANES)
-                d = got_qd[1, rows, at].reshape(HALF * TILE, LANES)
-                k = got_kv[0, spans, near].reshape(SPAN * TWIDE, LANES)
-                v = got_kv[1, spans, near].reshape(SPAN * TWIDE, LANES)
-                dq, dk, dv = pair_grads(q, d, k, v, mask[half])
-                final_q[i, rows] = dq.astype(bf16).reshape(HALF, TILE, LANES)
-                acc[0, spans, near] += dk.reshape(SPAN, TWIDE, LANES)
-                acc[1, spans, near] += dv.reshape(SPAN, TWIDE, LANES)
-
-        last = by((1 - core) * COLS, TILE)
+    last = by((1 - core) * COLS, TILE)
+
+    def compute(i):
+        begin = by(tile_of(i, core) * TILE, TILE)
+        at, near = pl.ds(begin, TILE), pl.ds(begin, TWIDE)
+
+        def half_tile(half):
+            rows = slice(half * HALF, (half + 1) * HALF)
+            spans = slice(half * HALF, half * HALF + SPAN)
+            q = got_qd[0, rows, at].reshape(HALF * TILE, LANES)
+            d = got_qd[1, rows, at].reshape(HALF * TILE, LANES)
+            k = got_kv[0, spans, near].reshape(SPAN * TWIDE, LANES)
+            v = got_kv[1, spans, near].reshape(SPAN * TWIDE, LANES)
+            dq, dk, dv = pair_grads(q, d, k, v, mask[half])
+            final_q[i, rows] = dq.astype(bf16).reshape(HALF, TILE, LANES)
+            acc[0, spans, near] += dk.reshape(SPAN, TWIDE, LANES)
+            acc[1, spans, near] += dv.reshape(SPAN, TWIDE, LANES)
 
         def send_edge(way):
             rows = (slice(0, RADIUS), slice(TALL - RADIUS, TALL))[way]
-            edge_out[u, way] = acc[:, rows, pl.ds(done_at(u), STEP)].astype(bf16)
-            edge(u, way).start()
-
-            @pl.when(u == STAGES - 1)
+            edge_out[i, way] = acc[:, rows, pl.ds(done_at(i), TILE)].astype(bf16)
+            edge(i, way).start()
+
+            @pl.when(i == TILES - 1)
             def _():
                 last_out[way] = acc[:, rows, pl.ds(last, TILE)].astype(bf16)
                 last_edge(way).start()
 
+        @pl.when((i % 2 == 0) & has_above)
+        def _():
+            relay_wait(i // 2, 1)
+
+        half_tile(0)
+
         @pl.when(has_above)
         def _():
-            relay_wait(u, 1)
-
-        tiles(0)
-
-        @pl.when(has_above)
-        def _():
             send_edge(0)
 
+        @pl.when((i % 2 == 0) & has_below)
+        def _():
+            relay_wait(i // 2, 0)
+
+        half_tile(1)
+
         @pl.when(has_below)
         def _():
-            relay_wait(u, 0)
-
-        tiles(1)
-
-        @pl.when(has_below)
-        def _():
             send_edge(1)
 
-        hand_out(q_pair, 2 * u, q_gone, q_came)
-        hand_out(q_pair, 2 * u + 1, q_gone, q_came)
-
-    def add_edges(u):
-        last = by((1 - core) * COLS, TILE)
-
+    def add_edges(i):
         def add(way):
             rows = (slice(ROWS, ROWS + RADIUS), slice(RADIUS, 2 * RADIUS))[way]
-            edge(u, way).wait_recv()
-            acc[:, rows, pl.ds(done_at(u), STEP)] += edge_in[u, way].astype(f32)
-
-            @pl.when(u == STAGES - 1)
+            edge(i, way).wait_recv()
+            acc[:, rows, pl.ds(done_at(i), TILE)] += edge_in[i, way].astype(f32)
+
+            @pl.when(i == TILES - 1)
             def _():
                 last_edge(way).wait_recv()
                 acc[:, rows, pl.ds(last, TILE)] += last_in[way].astype(f32)
@@ -365,63 +362,71 @@
         def _():
             add(1)
 
-        def send_side(i, at):
+        def send_side(n, at):
             cols = pl.ds(by(at, SIDE), SIDE)
-            side_out[i] = jnp.concatenate([acc[0, own, cols], acc[1, own, cols]], axis=1).astype(bf16)
-            side(i).start()
-
-        @pl.when(u == 0)
+            side_out[n] = jnp.concatenate([acc[0, own, cols], acc[1, own, cols]], axis=1).astype(bf16)
+            side(n).start()
+
+        @pl.when(i == 0)
         def _():
             send_side(0, core * (WIDE - SIDE))
 
-        @pl.when(u == STAGES - 1)
+        @pl.when(i == TILES - 1)
         def _():
             send_side(1, (1 - core) * (WIDE - SIDE))
 
-        @pl.when(u > 0)
-        def _():
-            hand_out_kv(2 * u - 1)
-            hand_out_kv(2 * u)
-
-    def add_side(i, at, tile):
-        side(i).wait_recv()
+    def add_side(n, at):
+        side(n).wait_recv()
         cols = pl.ds(by(at, SIDE), SIDE)
-        got = side_in[i].astype(f32)
+        got = side_in[n].astype(f32)
         acc[0, own, cols] += got[:, :SIDE]
         acc[1, own, cols] += got[:, SIDE:]
-        hand_out_kv(tile)
-
-    @pl.loop(0, STAGES + 1)
+
+    @pl.loop(0, TILES)
     def _(i):
-        @pl.when(i < STAGES)
-        def _():
-            pass_keys(i)
+        @pl.when(i == 0)
+        def _():
+            pass_keys(0)
+
+        @pl.when(i % 2 == 1)
+        def _():
+            @pl.when(i < TILES - 1)
+            def _():
+                pass_keys(i // 2 + 1)
+
+        own_wait(own_qd, i, got_qd, TILE)
+        came_wait(came_qd, i, got_qd, TILE)
+
+        compute(i)
+        hand_out(q_pair, i, q_gone, q_came)
+
+        @pl.when(i > 0)
+        def _():
+            add_edges(i - 1)
 
         @pl.when(i == 2)
         def _():
-            add_side(0, either(core, SIDE, COLS), 0)
-
-        @pl.when(i > 0)
-        def _():
-            add_edges(i - 1)
-
-        @pl.when(i < STAGES)
-        def _():
-            compute(i)
-
-    add_side(1, either(core, COLS, SIDE), TILES - 1)
+            add_side(0, either(core, SIDE, COLS))
+
+        @pl.when(i > 1)
+        def _():
+            finish_kv(i - 2)
+            hand_out(kv_pair, i - 2, kv_gone, kv_came)
+
+    add_edges(TILES - 1)
+    finish_kv(TILES - 2)
+    hand_out(kv_pair, TILES - 2, kv_gone, kv_came)
+    add_side(1, either(core, COLS, SIDE))
+    finish_kv(TILES - 1)
+    hand_out(kv_pair, TILES - 1, kv_gone, kv_came)
 
     came_wait(sent_kv, 0, got_kv, 3 * TILE)
-    came_wait(sent_qd, 0, got_qd, STEP)
     on_ways(lambda way: relay(0, way, True), lambda copy: copy.wait_send())
-    on_ways(lambda way: edge(0, way), lambda copy: copy.wait_send())
-
-    @pl.loop(1, STAGES)
+
+    @pl.loop(1, PARTS)
     def _(u):
         came_wait(sent_kv, u, got_kv, STEP)
-        came_wait(sent_qd, u, got_qd, STEP)
         on_ways(lambda way: relay(u, way, False), lambda copy: copy.wait_send())
-        on_ways(lambda way: edge(u, way), lambda copy: copy.wait_send())
 
     on_ways(last_edge, lambda copy: copy.wait_send())
     side(0).wait_send()
@@ -429,6 +434,8 @@
 
     @pl.loop(0, TILES)
     def _(i):
+        came_wait(sent_qd, i, got_qd, TILE)
+        on_ways(lambda way: edge(i, way), lambda copy: copy.wait_send())
         hand_out_wait(q_pair, i, q_gone)
         hand_out_wait(kv_pair, i, kv_gone)
         for pair, came in ((q_pair, q_came), (kv_pair, kv_came)):
@@ -454,16 +461,16 @@
             vmem(2, ROWS, COLS, LANES),
             pltpu.VMEM((2, SPAN * TWIDE, 2 * HALF * TILE), f32),
             pltpu.VMEM((2, TALL, WIDE, LANES), f32),
-            vmem(STAGES, 2, 2, RADIUS, STEP, LANES),
-            vmem(STAGES, 2, 2, RADIUS, STEP, LANES),
+            vmem(TILES, 2, 2, RADIUS, TILE, LANES),
+            vmem(TILES, 2, 2, RADIUS, TILE, LANES),
             vmem(2, 2, RADIUS, TILE, LANES),
             vmem(2, 2, RADIUS, TILE, LANES),
             vmem(2, ROWS, 2 * SIDE, LANES),
             vmem(2, ROWS, 2 * SIDE, LANES),
             vmem(TILES, ROWS, TILE, LANES),
             vmem(TILES, 2, ROWS, TILE, LANES),
-            sems(4), sems(STAGES), sems(STAGES), sems(STAGES), sems(STAGES), sems(STAGES, 2),
-            sems(STAGES, 2), sems(STAGES, 2), sems(STAGES + 1, 2), sems(STAGES + 1, 2), sems(2), sems(2),
+            sems(4), sems(PARTS), sems(TILES), sems(PARTS), sems(TILES), sems(PARTS), sems(TILES),
+            sems(PARTS, 2), sems(PARTS, 2), sems(TILES + 1, 2), sems(TILES + 1, 2), sems(2), sems(2),
             sems(TILES), sems(TILES), sems(TILES), sems(TILES),
         ],
         compiler_params=pltpu.CompilerParams(collective_id=0, has_side_effects=True, vmem_limit_bytes=56 * 1024 * 1024),

time: 67.6 us -> 62.1 us (0.919)
  the two profiles are of different devices: /device:TPU:25 before, /device:TPU:24 now
where the time goes in v4:
time: 62.1 us; the launch traced here: 61.9 us
  Pallas kernels  58.7 us (95%)
  local copies, waits for them, and re-layouts  2.54 us (4%)
  between operations  0.64 us (1%)
    pallas_call x1, Pallas kernels, on_device(): pl.pallas_call(functools.partial(kernel, lats), out_shape=jax.ShapeDtypeS...  58.7 us
    squeeze x1, local copies, waits for them, and re-layouts, on_device(): return (out[0], out[1], out[2])  2.54 us

profile of v4, /device:TPU:24, one launch (start us, length us, event | category | flops | bytes accessed | tf_op | source)
XLA Modules:
  0.0 61.9 jit_solution(13838259570322484702)
XLA Ops:
  0.6 58.7 %shard_map.67 = bf16[3,16,16,1024]{3,2,1,0:T(8,128)(2,1)} custom-call(bf16[1,256,1024]{2,1,0:T(8,128)(2,1)} %q_ref.1, bf16[1,256,1024]{2,1,0:T(8,128)(2,1)} %k_ref.1, bf16[1,256,1024]{2,1,0:T(8,128)(2,1)} %v_ref.1, bf16[1,256,1024]{2,1,0:T(8,128)(2,1)} %d_ref.1), custom_call_target="tpu_custom_call" | custom-call | tf_op jit(solution)/shard_map/pallas_call | solution.py:451
  59.4 2.5 %slice_bitcast_fusion = (bf16[16,16,1024]{2,1,0:T(8,128)(2,1)}, bf16[16,16,1024]{2,1,0:T(8,128)(2,1)}, bf16[16,16,1024]{2,1,0:T(8,128)(2,1)}) fusion(bf16[3,16,16,1024]{3,2,1,0:T(8,128)(2,1)} %shard_map.67), kind=kLoop, calls=%fused_computation | loop fusion | bytes 3145728 | tf_op jit(solution)/shard_map/squeeze | solution.py:478

commit v5 on v4

--- a/solution.py
+++ b/solution.py
@@ -170,16 +170,16 @@
         spread(qd_copy, i, sent_qd, came_qd, own_qd)
 
     spread_kv(0, True)
-    spread_qd(0)
 
     @pl.loop(1, PARTS)
     def _(u):
         spread_kv(u)
 
-        @pl.loop(2 * u - 1, 2 * u + 1)
+        @pl.loop(2 * u - 2, 2 * u)
         def _(i):
             spread_qd(i)
 
+    spread_qd(TILES - 2)
     spread_qd(TILES - 1)
 
     for half in range(2):
@@ -388,11 +388,9 @@
         def _():
             pass_keys(0)
 
-        @pl.when(i % 2 == 1)
-        def _():
-            @pl.when(i < TILES - 1)
-            def _():
-                pass_keys(i // 2 + 1)
+        @pl.when((i % 2 == 0) & (i < TILES - 2))
+        def _():
+            pass_keys(i // 2 + 1)
 
         own_wait(own_qd, i, got_qd, TILE)
         came_wait(came_qd, i, got_qd, TILE)
@@ -400,19 +398,22 @@
         compute(i)
         hand_out(q_pair, i, q_gone, q_came)
 
-        @pl.when(i > 0)
-        def _():
-            add_edges(i - 1)
-
-        @pl.when(i == 2)
+        @pl.when(i > 1)
+        def _():
+            add_edges(i - 2)
+
+        @pl.when(i == 3)
         def _():
             add_side(0, either(core, SIDE, COLS))
 
-        @pl.when(i > 1)
-        def _():
-            finish_kv(i - 2)
-            hand_out(kv_pair, i - 2, kv_gone, kv_came)
-
+        @pl.when(i > 2)
+        def _():
+            finish_kv(i - 3)
+            hand_out(kv_pair, i - 3, kv_gone, kv_came)
+
+    add_edges(TILES - 2)
+    finish_kv(TILES - 3)
+    hand_out(kv_pair, TILES - 3, kv_gone, kv_came)
     add_edges(TILES - 1)
     finish_kv(TILES - 2)
     hand_out(kv_pair, TILES - 2, kv_gone, kv_came)

time: 62.1 us -> 56 us (0.902)
  the two profiles are of different devices: /device:TPU:24 before, /device:TPU:80 now
where the time goes in v5:
time: 56 us; the launch traced here: 55.8 us
  Pallas kernels  52.7 us (94%)
  local copies, waits for them, and re-layouts  2.54 us (5%)
  between operations  0.64 us (1%)
    pallas_call x1, Pallas kernels, on_device(): pl.pallas_call(functools.partial(kernel, lats), out_shape=jax.ShapeDtypeS...  52.7 us
    squeeze x1, local copies, waits for them, and re-layouts, on_device(): return (out[0], out[1], out[2])  2.54 us

profile of v5, /device:TPU:80, one launch (start us, length us, event | category | flops | bytes accessed | tf_op | source)
XLA Modules:
  0.0 55.8 jit_solution(16054478238778755882)
XLA Ops:
  0.6 52.7 %shard_map.67 = bf16[3,16,16,1024]{3,2,1,0:T(8,128)(2,1)} custom-call(bf16[1,256,1024]{2,1,0:T(8,128)(2,1)} %q_ref.1, bf16[1,256,1024]{2,1,0:T(8,128)(2,1)} %k_ref.1, bf16[1,256,1024]{2,1,0:T(8,128)(2,1)} %v_ref.1, bf16[1,256,1024]{2,1,0:T(8,128)(2,1)} %d_ref.1), custom_call_target="tpu_custom_call" | custom-call | tf_op jit(solution)/shard_map/pallas_call | solution.py:452
  53.3 2.5 %slice_bitcast_fusion = (bf16[16,16,1024]{2,1,0:T(8,128)(2,1)}, bf16[16,16,1024]{2,1,0:T(8,128)(2,1)}, bf16[16,16,1024]{2,1,0:T(8,128)(2,1)}) fusion(bf16[3,16,16,1024]{3,2,1,0:T(8,128)(2,1)} %shard_map.67), kind=kLoop, calls=%fused_computation | loop fusion | bytes 3145728 | tf_op jit(solution)/shard_map/squeeze | solution.py:479

commit v6 on v5

--- a/solution.py
+++ b/solution.py
@@ -15,6 +15,7 @@
 ROWS = 16
 TILE = 16
 TILES = 8
+PIECES = 4
 PARTS = 4
 STEP = 2 * TILE
 COLS = TILES * TILE
@@ -98,7 +99,7 @@
     above, below = neighbour(lat - more_above), neighbour(lat + more_below)
 
     def start_block(g, c):
-        return (2 * g + (DEVICES // 2) * c) % DEVICES
+        return (2 * g + 10 + (DEVICES // 2) * c) % DEVICES
 
     def other(hop):
         ox, oz, oc = (x + hop[0]) % 4, (z + hop[1]) % 2, (core + hop[2]) % 2
@@ -106,8 +107,6 @@
 
     loads = [pltpu.make_async_copy(r.at[0], t, load_sem.at[i]) for i, (r, t) in enumerate(
         ((k_ref, raw.at[0]), (v_ref, raw.at[1]), (q_ref, send_qd.at[0]), (d_ref, send_qd.at[1])))]
-    for load in loads:
-        load.start()
 
     barrier = pltpu.get_barrier_semaphore()
     for hop in HOPS:
@@ -120,6 +119,9 @@
     @pl.when(has_below)
     def _():
         pl.semaphore_signal(barrier, inc=1, device_id=below, device_id_type=MESH)
+
+    for load in loads:
+        load.start()
 
     def kv_at(u, c):
         return either(c, 16 + STEP * u, 96 - STEP * u)
@@ -442,6 +444,21 @@
         for pair, came in ((q_pair, q_came), (kv_pair, kv_came)):
             src, dst = pair(i)
             pltpu.make_async_copy(src, dst, came.at[i]).wait()
+
+
+def part_kernel(all_ref, *refs):
+    outs, (held, load_sem, store_sem) = refs[:3], refs[3:]
+    size = ROWS // PIECES
+    pairs = [(i, j, slice(j * size, (j + 1) * size)) for i in range(3) for j in range(PIECES)]
+    loads = [pltpu.make_async_copy(all_ref.at[i, s], held.at[i, s], load_sem.at[i, j]) for i, j, s in pairs]
+    stores = [pltpu.make_async_copy(held.at[i, s], outs[i].at[s], store_sem.at[i, j]) for i, j, s in pairs]
+    for load in loads:
+        load.start()
+    for load, store in zip(loads, stores):
+        load.wait()
+        store.start()
+    for store in stores:
+        store.wait()
 
 
 def on_device(queries, keys, values, grads_out):
@@ -476,7 +493,14 @@
         ],
         compiler_params=pltpu.CompilerParams(collective_id=0, has_side_effects=True, vmem_limit_bytes=56 * 1024 * 1024),
     )(queries, keys, values, grads_out)
-    return out[0], out[1], out[2]
+    shape = jax.ShapeDtypeStruct(out.shape[1:], bf16)
+    return pl.pallas_call(
+        part_kernel,
+        in_specs=[pl.BlockSpec(memory_space=pl.ANY)],
+        out_specs=[pl.BlockSpec(memory_space=pl.ANY)] * 3,
+        out_shape=[shape] * 3,
+        scratch_shapes=[pltpu.VMEM(out.shape, bf16), sems(3, PIECES), sems(3, PIECES)],
+    )(out)
 
 
 def solution(mesh):

time: 56 us -> 54.8 us (0.979)
  the two profiles are of different devices: /device:TPU:80 before, /device:TPU:25 now
where the time goes in v6:
time: 54.8 us; the launch traced here: 54.1 us
  Pallas kernels  53.4 us (97%)
  between operations  0.64 us (1%)
    pallas_call x1, Pallas kernels, on_device(): pl.pallas_call(functools.partial(kernel, lats), out_shape=jax.ShapeDtypeS...  51.1 us
    pallas_call x1, Pallas kernels, on_device(): pl.pallas_call(part_kernel, in_specs=[pl.BlockSpec(memory_space=pl.ANY)],...  2.33 us

profile of v6, /device:TPU:25, one launch (start us, length us, event | category | flops | bytes accessed | tf_op | source)
XLA Modules:
  0.0 54.1 jit_solution(153480631338717377)
XLA Ops:
  0.6 51.1 %shard_map.67.all_ref = bf16[3,16,16,1024]{3,2,1,0:T(8,128)(2,1)} custom-call(bf16[1,256,1024]{2,1,0:T(8,128)(2,1)} %q_ref.1, bf16[1,256,1024]{2,1,0:T(8,128)(2,1)} %k_ref.1, bf16[1,256,1024]{2,1,0:T(8,128)(2,1)} %v_ref.1, bf16[1,256,1024]{2,1,0:T(8,128)(2,1)} %d_ref.1), custom_call_target="tpu_custom_call" | custom-call | tf_op jit(solution)/shard_map/pallas_call | solution.py:469
  51.7 2.3 %shard_map.68 = (bf16[16,16,1024]{2,1,0:T(8,128)(2,1)}, bf16[16,16,1024]{2,1,0:T(8,128)(2,1)}, bf16[16,16,1024]{2,1,0:T(8,128)(2,1)}) custom-call(bf16[3,16,16,1024]{3,2,1,0:T(8,128)(2,1)} %shard_map.67.all_ref), custom_call_target="tpu_custom_call" | custom-call | tf_op jit(solution)/shard_map/pallas_call | solution.py:497

commit v7 on v6

--- a/solution.py
+++ b/solution.py
@@ -70,8 +70,8 @@
     return jnp.where(first, dq[:count], dq[count:]), dk, dv
 
 
-HOPS = [(1, 0, 0), (3, 0, 0), (0, 1, 0), (2, 0, 0), (1, 1, 0), (3, 1, 0), (0, 1, 1), (2, 1, 0), (1, 0, 1),
-        (3, 0, 1), (2, 0, 1), (1, 1, 1), (3, 1, 1), (2, 1, 1), (0, 0, 1)]
+HOPS = [(2, 1, 0), (1, 0, 0), (3, 0, 1), (2, 0, 1), (0, 1, 0), (1, 1, 1), (3, 1, 0), (2, 0, 0), (2, 1, 1),
+        (1, 0, 1), (3, 0, 0), (0, 1, 1), (1, 1, 0), (3, 1, 1), (0, 0, 1)]
 
 
 def either(core, a, b):

time: 54.8 us -> 54.9 us (level)
  no operation moved by 1% of the time
where the time goes in v7:
time: 54.9 us; the launch traced here: 53.9 us
  Pallas kernels  53.3 us (97%)
  between operations  0.64 us (1%)
    pallas_call x1, Pallas kernels, on_device(): pl.pallas_call(functools.partial(kernel, lats), out_shape=jax.ShapeDtypeS...  51 us
    pallas_call x1, Pallas kernels, on_device(): pl.pallas_call(part_kernel, in_specs=[pl.BlockSpec(memory_space=pl.ANY)],...  2.33 us

profile of v7, /device:TPU:25, one launch (start us, length us, event | category | flops | bytes accessed | tf_op | source)
XLA Modules:
  0.0 53.9 jit_solution(17447548996266137269)
XLA Ops:
  0.6 51.0 %shard_map.67.all_ref = bf16[3,16,16,1024]{3,2,1,0:T(8,128)(2,1)} custom-call(bf16[1,256,1024]{2,1,0:T(8,128)(2,1)} %q_ref.1, bf16[1,256,1024]{2,1,0:T(8,128)(2,1)} %k_ref.1, bf16[1,256,1024]{2,1,0:T(8,128)(2,1)} %v_ref.1, bf16[1,256,1024]{2,1,0:T(8,128)(2,1)} %d_ref.1), custom_call_target="tpu_custom_call" | custom-call | tf_op jit(solution)/shard_map/pallas_call | solution.py:469
  51.6 2.3 %shard_map.68 = (bf16[16,16,1024]{2,1,0:T(8,128)(2,1)}, bf16[16,16,1024]{2,1,0:T(8,128)(2,1)}, bf16[16,16,1024]{2,1,0:T(8,128)(2,1)}) custom-call(bf16[3,16,16,1024]{3,2,1,0:T(8,128)(2,1)} %shard_map.67.all_ref), custom_call_target="tpu_custom_call" | custom-call | tf_op jit(solution)/shard_map/pallas_call | solution.py:497

commit v8 on v6

--- a/solution.py
+++ b/solution.py
@@ -139,8 +139,6 @@
             a = raw[i, :, lanes].astype(f32)
             a = jnp.concatenate([a[-SIDE:], a, a[:STEP - SIDE]], axis=0)
             shifted[i, :, lanes] = a.astype(bf16)
-    loads[2].wait()
-    loads[3].wait()
 
     pl.semaphore_wait(barrier, OTHERS + more_above + more_below)
 
@@ -172,8 +170,13 @@
         spread(qd_copy, i, sent_qd, came_qd, own_qd)
 
     spread_kv(0, True)
-
-    @pl.loop(1, PARTS)
+    spread_kv(1)
+    loads[2].wait()
+    loads[3].wait()
+    spread_qd(0)
+    spread_qd(1)
+
+    @pl.loop(2, PARTS)
     def _(u):
         spread_kv(u)
 

time: 54.8 us -> 54.8 us (level)
  no operation moved by 1% of the time
where the time goes in v8:
time: 54.8 us; the launch traced here: 54.1 us
  Pallas kernels  53.4 us (97%)
  between operations  0.64 us (1%)
    pallas_call x1, Pallas kernels, on_device(): pl.pallas_call(functools.partial(kernel, lats), out_shape=jax.ShapeDtypeS...  51.1 us
    pallas_call x1, Pallas kernels, on_device(): pl.pallas_call(part_kernel, in_specs=[pl.BlockSpec(memory_space=pl.ANY)],...  2.33 us

profile of v8, /device:TPU:25, one launch (start us, length us, event | category | flops | bytes accessed | tf_op | source)
XLA Modules:
  0.0 54.1 jit_solution(5836039384530627378)
XLA Ops:
  0.6 51.1 %shard_map.67.all_ref = bf16[3,16,16,1024]{3,2,1,0:T(8,128)(2,1)} custom-call(bf16[1,256,1024]{2,1,0:T(8,128)(2,1)} %q_ref.1, bf16[1,256,1024]{2,1,0:T(8,128)(2,1)} %k_ref.1, bf16[1,256,1024]{2,1,0:T(8,128)(2,1)} %v_ref.1, bf16[1,256,1024]{2,1,0:T(8,128)(2,1)} %d_ref.1), custom_call_target="tpu_custom_call" | custom-call | tf_op jit(solution)/shard_map/pallas_call | solution.py:472
  51.7 2.3 %shard_map.68 = (bf16[16,16,1024]{2,1,0:T(8,128)(2,1)}, bf16[16,16,1024]{2,1,0:T(8,128)(2,1)}, bf16[16,16,1024]{2,1,0:T(8,128)(2,1)}) custom-call(bf16[3,16,16,1024]{3,2,1,0:T(8,128)(2,1)} %shard_map.67.all_ref), custom_call_target="tpu_custom_call" | custom-call | tf_op jit(solution)/shard_map/pallas_call | solution.py:500
